TPU v7x, 128 devices: a whole 4x4x4 slice. The times are simulated.
128 devices in a mesh: tm: 16 (over x, y_hi, core), head: 8 (over y_lo, z).
Axes of the slice: x: 4, y: 4 (y_hi: 2, y_lo: 2; y = y_hi * 2 + y_lo), z: 4, core: 2. Of those that a mesh axis runs over, the one named last changes fastest.
Arguments:
- q_in: bfloat16 [16, 1536, 5120], P('tm', 'head'), may hold values from -256 to 256
- k_in: bfloat16 [16, 1536, 5120], P('tm', 'head'), may hold values from -256 to 256
- v_in: bfloat16 [16, 1536, 5120], P('tm', 'head'), may hold values from -6 to 6
- q_gain: float32 [5120], replicated, may hold values from 0.5 to 2
- k_gain: float32 [5120], replicated, may hold values from 0.5 to 2
- keep_one: int32 [16, 2, 6], replicated, may hold values from 0 to 11, as said below
- keep_two: int32 [16, 2, 3], replicated, may hold values from 0 to 11, as said below
- keep_four: int32 [16, 2, 1], replicated, may hold values from 0 to 11, as said below
- keep_eight: int32 [16, 2, 1], replicated, may hold values from 0 to 11, as said below
Outputs:
- attended: bfloat16 [16, 1536, 5120], P('tm', 'head')
Inputs may be any that keep to these rules, and one draw needn't show every extreme that they name: `keep_one`: each row lists distinct block numbers of a frame in increasing order. `keep_two`: each row lists distinct block numbers of a frame in increasing order. `keep_four`: each row lists distinct block numbers of a frame in increasing order. `keep_eight`: each row lists distinct block numbers of a frame in increasing order.
All inputs are finite; a program needn't handle non-finite values.
Results may differ from a plain program's by a relative error of at most 0.0025.
The roundings to bfloat16 on the way count: a program that leaves them out, or rounds other values in their place, can miss the bound.
Values may be sent and summed in bfloat16 or wider, within the bound.
A program may use at most 192 MiB of HBM per device.

v0:
```python
import math

import jax
import jax.numpy as jnp
from jax import lax
from jax.sharding import PartitionSpec as P

HEADS = 40
BLK = 128


EPSILON = 1e-06
NEGATIVE = -1e30


def passed_along(value, axis, steps):
    count = lax.axis_size(axis)
    first, last = (max(0, -steps), min(count, count - steps))
    return lax.ppermute(value, axis, [(source, source + steps) for source in range(first, last)])


def normalize(values, gain):
    wide = values.astype(jnp.float32)
    meansq = jnp.mean(wide * wide, axis=-1, keepdims=True)
    return (wide * lax.rsqrt(meansq + EPSILON) * gain).astype(jnp.bfloat16)


def on_device(q_in, k_in, v_in, q_gain, k_gain, keep_one, keep_two, keep_four, keep_eight):
    groups = lax.axis_size("head")
    local_tokens = q_in.shape[1]
    width = q_in.shape[2]
    per_group = HEADS // groups
    head_size = width // HEADS
    queries = normalize(q_in[0], q_gain).reshape(local_tokens, groups, per_group, head_size)
    key_rows = normalize(k_in[0], k_gain).reshape(local_tokens, groups, per_group, head_size)
    value_rows = v_in[0].reshape(local_tokens, groups, per_group, head_size)
    keeps = ((1, keep_one), (2, keep_two), (4, keep_four), (8, keep_eight))
    query_part = lax.all_to_all(queries, "head", split_axis=1, concat_axis=0, tiled=True)
    key_part = lax.all_to_all(key_rows, "head", split_axis=1, concat_axis=0, tiled=True)
    value_part = lax.all_to_all(value_rows, "head", split_axis=1, concat_axis=0, tiled=True)
    total_tokens = query_part.shape[0]
    count_heads = query_part.shape[2]
    own_queries = query_part[:, 0]
    own_keys = key_part[:, 0]
    own_values = value_part[:, 0]
    frame = lax.axis_index("tm")
    frames = lax.axis_size("tm")
    blocks = total_tokens // BLK
    paired = jnp.stack([own_keys, own_values]).reshape(2, blocks, BLK, count_heads, head_size)
    key_parts = [own_keys]
    value_parts = [own_values]
    usable_parts = [jnp.ones((total_tokens,), dtype=bool)]
    for distance, keep in keeps:
        kept_count = keep.shape[2]
        for direction in (0, 1):
            if direction == 0:
                target = jnp.minimum(frame + distance, frames - 1)
            else:
                target = jnp.maximum(frame - distance, 0)
            rows = lax.dynamic_index_in_dim(keep, target, 0, keepdims=False)
            packed = jnp.take(paired, rows[direction], axis=1).reshape(
                2, kept_count * BLK, count_heads, head_size
            )
            if direction == 0:
                arrived = passed_along(packed, "tm", distance)
                inside = frame - distance >= 0
            else:
                arrived = passed_along(packed, "tm", -distance)
                inside = frame + distance < frames
            key_parts.append(arrived[0])
            value_parts.append(arrived[1])
            usable_parts.append(jnp.full((kept_count * BLK,), inside))
    keys_all = jnp.concatenate(key_parts, axis=0)
    values_all = jnp.concatenate(value_parts, axis=0)
    usable = jnp.concatenate(usable_parts, axis=0)
    scale = 1.0 / math.sqrt(head_size)
    block_rows = math.gcd(total_tokens, 512)
    query_blocks = own_queries.reshape(
        total_tokens // block_rows, block_rows, count_heads, head_size
    )

    def one_block(block):
        scores = (
            jnp.einsum("qhd,khd->hqk", block, keys_all, preferred_element_type=jnp.float32) * scale
        )
        scores = jnp.where(usable[None, None, :], scores, NEGATIVE)
        top = jnp.max(scores, axis=-1, keepdims=True)
        expo = jnp.exp(scores - top)
        totals = jnp.sum(expo, axis=-1, keepdims=True)
        weights = expo.astype(jnp.bfloat16)
        summed = jnp.einsum("hqk,khd->qhd", weights, values_all, preferred_element_type=jnp.float32)
        return (summed / jnp.transpose(totals, (1, 0, 2))).astype(jnp.bfloat16)

    result = lax.map(one_block, query_blocks)
    outputs = result.reshape(total_tokens, 1, count_heads, head_size)
    gathered = lax.all_to_all(outputs, "head", split_axis=0, concat_axis=1, tiled=True)
    return gathered.reshape(1, local_tokens, width)


def solution(mesh):
    return jax.shard_map(
        on_device,
        mesh=mesh,
        in_specs=(
            P("tm", "head", None),
            P("tm", "head", None),
            P("tm", "head", None),
            P(),
            P(),
            P(),
            P(),
            P(),
            P(),
        ),
        out_specs=P("tm", "head", None),
        check_vma=False,
    )
```

profile of v0, /device:TPU:2, one launch (start us, length us, event | category | flops | bytes accessed | tf_op | source)
XLA Modules:
  0.0 419.7 jit_solution(3361943522866796496)
XLA Ops:
  0.0 4.8 %copy.47 = f32[1,192,5120]{1,2,0:T(8,128)} copy(bf16[1,192,5120]{2,1,0:T(8,128)(2,1)} %param.18) | data formatting | bytes 5898240 | tf_op jit(solution)/shard_map/convert_element_type | solution.py:23
  5.4 3.0 multiply_convert_fusion
  8.3 2.4 copy.48
  10.8 6.3 %all-to-all-start.1 = ((bf16[192,8,5,128]{3,0,2,1:T(8,128)(2,1)}), bf16[192,8,5,128]{3,0,2,1:T(8,128)(2,1)}, u32[]{:S(2)}, u32[]{:S(2)}) async-start(bf16[192,8,5,128]{3,0,2,1:T(8,128)(2,1)} %copy.48), calls=%async_computation.1 | async-start | bytes 3932160 | tf_op jit(solution)/shard_map/all_to_all | solution.py:39
  17.1 2.8 copy.50
  20.0 2.5 copy.51
  22.4 19.4 %all-to-all-done.1 = bf16[192,8,5,128]{3,0,2,1:T(8,128)(2,1)} async-done(((bf16[192,8,5,128]{3,0,2,1:T(8,128)(2,1)}), bf16[192,8,5,128]{3,0,2,1:T(8,128)(2,1)}, u32[]{:S(2)}, u32[]{:S(2)}) %all-to-all-start.1) | async-done | bytes 1966112 | tf_op jit(solution)/shard_map/all_to_all | solution.py:39
  41.8 4.4 %all-to-all-start.2 = ((bf16[192,8,5,128]{3,0,2,1:T(8,128)(2,1)}), bf16[192,8,5,128]{3,0,2,1:T(8,128)(2,1)}, u32[]{:S(2)}, u32[]{:S(2)}) async-start(bf16[192,8,5,128]{3,0,2,1:T(8,128)(2,1)} %copy.51), calls=%async_computation.2 | async-start | bytes 3932160 | tf_op jit(solution)/shard_map/all_to_all | solution.py:40
  54.6 3.2 copy.44
  58.3 3.0 multiply_convert_fusion.1
  61.3 2.5 copy.45
  68.3 2.6 all-to-all-done.2
  70.9 4.3 %all-to-all-start = ((bf16[192,8,5,128]{3,0,2,1:T(8,128)(2,1)}), bf16[192,8,5,128]{3,0,2,1:T(8,128)(2,1)}, u32[]{:S(2)}, u32[]{:S(2)}) async-start(bf16[192,8,5,128]{3,0,2,1:T(8,128)(2,1)} %copy.45), calls=%async_computation | async-start | bytes 3932160 | tf_op jit(solution)/shard_map/all_to_all | solution.py:38
  78.6 2.1 copy.65
  80.7 4.3 %gather_fusion = bf16[6,2,128,5,128]{4,2,3,1,0:T(8,128)(2,1)} fusion(bf16[2,12,128,5,128]{4,2,3,0,1:T(8,128)(2,1)} %copy.65, s32[1024]{0:T(1024)S(1)} %pad_clamp_fusion.3), kind=kCustom, calls=%fused_computation.clone | custom fusion | bytes 3932184 | tf_op jit(solution)/shard_map/jit(_take)/gather | solution.py:61
  85.0 1.8 select_bitcast_fusion.1
  88.2 1.9 collective-permute-start
  90.2 4.3 %gather_fusion.1 = bf16[6,2,128,5,128]{4,2,3,1,0:T(8,128)(2,1)} fusion(bf16[2,12,128,5,128]{4,2,3,0,1:T(8,128)(2,1)} %copy.65, s32[1024]{0:T(1024)S(1)} %pad_clamp_fusion.2), kind=kCustom, calls=%fused_computation.2.clone | custom fusion | bytes 3932184 | tf_op jit(solution)/shard_map/jit(_take)/gather | solution.py:61
  94.5 1.8 select_bitcast_fusion
  97.8 6.0 %collective-permute-start.1 = (bf16[2,768,5,128]{3,1,2,0:T(8,128)(2,1)}, bf16[2,768,5,128]{3,1,2,0:T(8,128)(2,1)}, u32[]{:S(2)}, u32[]{:S(2)}) collective-permute-start(bf16[2,768,5,128]{3,1,2,0:T(8,128)(2,1)} %bitcast.27), channel_id=1, source_target_pairs={{8,0},{16,8},{24,16},{32,24},{40,32},{48,40},{56,48},{64,56},{72,6... | collective-permute-start | bytes 5898248 | tf_op jit(solution)/shard_map/ppermute | solution.py:19
  103.9 2.8 gather_fusion.2
  107.9 3.9 collective-permute-start.2
  111.8 2.8 gather_fusion.3
  115.9 4.3 %collective-permute-start.3 = (bf16[2,384,5,128]{3,1,2,0:T(8,128)(2,1)}, bf16[2,384,5,128]{3,1,2,0:T(8,128)(2,1)S(1)}, u32[]{:S(2)}, u32[]{:S(2)}) collective-permute-start(bf16[2,384,5,128]{3,1,2,0:T(8,128)(2,1)} %bitcast.33), channel_id=1, source_target_pairs={{16,0},{24,8},{32,16},{40,24},{48,32},{56,40},{64,48},{72,56},{80,... | collective-permute-start | bytes 2949128 | tf_op jit(solution)/shard_map/ppermute | solution.py:19
  121.3 3.4 collective-permute-start.4
  124.7 2.7 constant_dynamic-update-slice_fusion
  129.2 3.3 collective-permute-start.5
  132.5 3.1 fusion.24
  135.7 3.3 collective-permute-start.6
  139.0 3.1 fusion.23
  142.1 27.4 %collective-permute-done.2 = bf16[2,384,5,128]{3,1,2,0:T(8,128)(2,1)} collective-permute-done((bf16[2,384,5,128]{3,1,2,0:T(8,128)(2,1)}, bf16[2,384,5,128]{3,1,2,0:T(8,128)(2,1)}, u32[]{:S(2)}, u32[]{:S(2)}) %collective-permute-start.2) | collective-permute-done | bytes 983072 | tf_op jit(solution)/shard_map/ppermute | solution.py:19
  170.7 2.3 fusion.28
  173.1 11.2 %collective-permute-done.3 = bf16[2,384,5,128]{3,1,2,0:T(8,128)(2,1)S(1)} collective-permute-done((bf16[2,384,5,128]{3,1,2,0:T(8,128)(2,1)}, bf16[2,384,5,128]{3,1,2,0:T(8,128)(2,1)S(1)}, u32[]{:S(2)}, u32[]{:S(2)}) %collective-permute-start.3) | collective-permute-done | bytes 983072 | tf_op jit(solution)/shard_map/ppermute | solution.py:19
  185.4 1.8 fusion.34
  189.6 174.5 %while.11 = (s32[]{:T(128)}, bf16[3,512,5,128]{3,1,0,2:T(8,128)(2,1)}, pred[4352]{0:T(1024)(128)(4,1)S(1)}, bf16[3,512,5,128]{3,1,0,2:T(8,128)(2,1)S(1)}, bf16[4...) while((s32[]{:T(128)}, bf16[3,512,5,128]{3,1,0,2:T(8,128)(2,1)}, ...), condition=%wide.region_5.9_spmd, body=%wide.region_2.8_spmd.sunk | while | flops 5827456000 | bytes 168493168 | solution.py:94
  189.6 20.0 %fusion.53 = (f32[5,512]{1,0:T(8,128)S(1)}, f32[5,512,4352]{2,1,0:T(8,128)}) fusion(pred[4352]{0:T(1024)(128)(4,1)S(1)} %get-tuple-element.181, bf16[4352,5,128]{2,0,1:T(8,128)(2,1)} %get-tuple-element.183, bf16[3,512,5,128]{3,1,0,2:T(8,128)(2,1)S(1)} %get-tuple-element.182, s32[]{:T(128)} %get-tuple-element.172), kind=kOutput, calls=%fused_computation.6.clone.1 | convolution fusion | flops 2885547520 | bytes 50805764 | tf_op jit(solution)/shard_map/while/body/eval_jaxpr/qhd,khd->hqk/dot_general | solution.py:84
  209.6 19.1 %fusion.54 = f32[5,512]{1,0:T(8,128)S(1)} fusion(f32[5,512,4352]{2,1,0:T(8,128)} %get-tuple-element.163, f32[5,512]{1,0:T(8,128)S(1)} %get-tuple-element.164, pred[4352]{0:T(1024)(128)(4,1)S(1)} %get-tuple-element.181), kind=kLoop, calls=%fused_computation.7.clone.1 | loop fusion | flops 44561920 | bytes 44589312 | tf_op jit(solution)/shard_map/while/body/eval_jaxpr/reduce_sum | solution.py:89
  228.7 19.1 %fusion.55 = bf16[3,512,5,128]{3,1,0,2:T(8,128)(2,1)} fusion(bf16[3,512,5,128]{3,1,0,2:T(8,128)(2,1)} %get-tuple-element.173, s32[]{:T(128)} %get-tuple-element.172, bf16[4352,5,128]{2,0,1:T(8,128)(2,1)S(1)} %copy-done.4, f32[5,512,4352]{2,1,0:T(8,128)} %get-tuple-element.163, f32[5,512]{1,0:T(8,128)S(1)} %get-tuple-element.164, ...), kind=kOutput, calls=%fused_computation.14.clone.1 | convolution fusion | flops 2897346560 | bytes 50815744 | tf_op jit(solution)/shard_map/while/body/eval_jaxpr/hqk,khd->qhd/dot_general | solution.py:91
  247.8 20.0 %fusion.53 = (f32[5,512]{1,0:T(8,128)S(1)}, f32[5,512,4352]{2,1,0:T(8,128)}) fusion(pred[4352]{0:T(1024)(128)(4,1)S(1)} %get-tuple-element.181, bf16[4352,5,128]{2,0,1:T(8,128)(2,1)} %get-tuple-element.183, bf16[3,512,5,128]{3,1,0,2:T(8,128)(2,1)S(1)} %get-tuple-element.182, s32[]{:T(128)} %get-tuple-element.172), kind=kOutput, calls=%fused_computation.6.clone.1 | convolution fusion | flops 2885547520 | bytes 50805764 | tf_op jit(solution)/shard_map/while/body/eval_jaxpr/qhd,khd->hqk/dot_general | solution.py:84
  267.8 19.1 %fusion.54 = f32[5,512]{1,0:T(8,128)S(1)} fusion(f32[5,512,4352]{2,1,0:T(8,128)} %get-tuple-element.163, f32[5,512]{1,0:T(8,128)S(1)} %get-tuple-element.164, pred[4352]{0:T(1024)(128)(4,1)S(1)} %get-tuple-element.181), kind=kLoop, calls=%fused_computation.7.clone.1 | loop fusion | flops 44561920 | bytes 44589312 | tf_op jit(solution)/shard_map/while/body/eval_jaxpr/reduce_sum | solution.py:89
  286.9 19.1 %fusion.55 = bf16[3,512,5,128]{3,1,0,2:T(8,128)(2,1)} fusion(bf16[3,512,5,128]{3,1,0,2:T(8,128)(2,1)} %get-tuple-element.173, s32[]{:T(128)} %get-tuple-element.172, bf16[4352,5,128]{2,0,1:T(8,128)(2,1)S(1)} %copy-done.4, f32[5,512,4352]{2,1,0:T(8,128)} %get-tuple-element.163, f32[5,512]{1,0:T(8,128)S(1)} %get-tuple-element.164, ...), kind=kOutput, calls=%fused_computation.14.clone.1 | convolution fusion | flops 2897346560 | bytes 50815744 | tf_op jit(solution)/shard_map/while/body/eval_jaxpr/hqk,khd->qhd/dot_general | solution.py:91
  305.9 20.0 %fusion.53 = (f32[5,512]{1,0:T(8,128)S(1)}, f32[5,512,4352]{2,1,0:T(8,128)}) fusion(pred[4352]{0:T(1024)(128)(4,1)S(1)} %get-tuple-element.181, bf16[4352,5,128]{2,0,1:T(8,128)(2,1)} %get-tuple-element.183, bf16[3,512,5,128]{3,1,0,2:T(8,128)(2,1)S(1)} %get-tuple-element.182, s32[]{:T(128)} %get-tuple-element.172), kind=kOutput, calls=%fused_computation.6.clone.1 | convolution fusion | flops 2885547520 | bytes 50805764 | tf_op jit(solution)/shard_map/while/body/eval_jaxpr/qhd,khd->hqk/dot_general | solution.py:84
  326.0 19.1 %fusion.54 = f32[5,512]{1,0:T(8,128)S(1)} fusion(f32[5,512,4352]{2,1,0:T(8,128)} %get-tuple-element.163, f32[5,512]{1,0:T(8,128)S(1)} %get-tuple-element.164, pred[4352]{0:T(1024)(128)(4,1)S(1)} %get-tuple-element.181), kind=kLoop, calls=%fused_computation.7.clone.1 | loop fusion | flops 44561920 | bytes 44589312 | tf_op jit(solution)/shard_map/while/body/eval_jaxpr/reduce_sum | solution.py:89
  345.1 19.1 %fusion.55 = bf16[3,512,5,128]{3,1,0,2:T(8,128)(2,1)} fusion(bf16[3,512,5,128]{3,1,0,2:T(8,128)(2,1)} %get-tuple-element.173, s32[]{:T(128)} %get-tuple-element.172, bf16[4352,5,128]{2,0,1:T(8,128)(2,1)S(1)} %copy-done.4, f32[5,512,4352]{2,1,0:T(8,128)} %get-tuple-element.163, f32[5,512]{1,0:T(8,128)S(1)} %get-tuple-element.164, ...), kind=kOutput, calls=%fused_computation.14.clone.1 | convolution fusion | flops 2897346560 | bytes 50815744 | tf_op jit(solution)/shard_map/while/body/eval_jaxpr/hqk,khd->qhd/dot_general | solution.py:91
  364.1 8.1 %copy.61 = bf16[1536,1,5,128]{3,2,1,0:T(8,128)(2,1)S(1)} copy(bf16[1536,1,5,128]{3,0,2,1:T(8,128)(2,1)} %bitcast.64) | data formatting | bytes 3932160 | tf_op jit(solution)/shard_map/reshape | solution.py:95
  372.3 40.6 %all_to_all.60 = bf16[1536,1,5,128]{3,2,1,0:T(8,128)(2,1)S(1)} all-to-all(bf16[1536,1,5,128]{3,2,1,0:T(8,128)(2,1)S(1)} %copy.61), channel_id=1, replica_groups=mesh['tm'=16,'head'=8] {'head'}, dimensions={0} | all-to-all | bytes 3932160 | tf_op jit(solution)/shard_map/all_to_all | solution.py:96
  414.4 2.9 copy.63
  417.3 2.4 copy.64
  (89 shorter events, 24.0 us)
Async XLA Ops:
  0.0 4.9 %copy-start.2 = (bf16[1,192,5120]{2,1,0:T(8,128)(2,1)S(1)}, bf16[1,192,5120]{2,1,0:T(8,128)(2,1)}, u32[]{:S(2)}) copy-start(bf16[1,192,5120]{2,1,0:T(8,128)(2,1)} %param.18) | copy-start | bytes 5898244
  0.0 5.3 %copy-start.6 = (f32[5120]{0:T(1024)S(1)}, f32[5120]{0:T(1024)}, u32[]{:S(2)}) copy-start(f32[5120]{0:T(1024)} %param.21) | copy-start | bytes 61444
  10.8 31.1 %all-to-all-start.1 = ((bf16[192,8,5,128]{3,0,2,1:T(8,128)(2,1)}), bf16[192,8,5,128]{3,0,2,1:T(8,128)(2,1)}, u32[]{:S(2)}, u32[]{:S(2)}) async-start(bf16[192,8,5,128]{3,0,2,1:T(8,128)(2,1)} %copy.48), calls=%async_computation.1 | async-start | bytes 3932160 | tf_op jit(solution)/shard_map/all_to_all | solution.py:39
  19.9 26.3 %copy-start.10 = (s32[16,2,1]{0,2,1:T(1,128)S(1)}, s32[16,2,1]{0,2,1:T(1,128)}, u32[]{:S(2)}) copy-start(s32[16,2,1]{0,2,1:T(1,128)} %param.25) | copy-start | bytes 388
  20.0 26.3 %copy-start.11 = (s32[16,2,1]{0,2,1:T(1,128)S(1)}, s32[16,2,1]{0,2,1:T(1,128)}, u32[]{:S(2)}) copy-start(s32[16,2,1]{0,2,1:T(1,128)} %param.24) | copy-start | bytes 388
  22.4 32.2 %copy-start.3 = (bf16[1,192,5120]{2,1,0:T(8,128)(2,1)S(1)}, bf16[1,192,5120]{2,1,0:T(8,128)(2,1)}, u32[]{:S(2)}) copy-start(bf16[1,192,5120]{2,1,0:T(8,128)(2,1)} %param.17) | copy-start | bytes 5898244
  22.4 35.4 %copy-start.7 = (f32[5120]{0:T(1024)S(1)}, f32[5120]{0:T(1024)}, u32[]{:S(2)}) copy-start(f32[5120]{0:T(1024)} %param.20) | copy-start | bytes 61444
  41.8 29.1 %all-to-all-start.2 = ((bf16[192,8,5,128]{3,0,2,1:T(8,128)(2,1)}), bf16[192,8,5,128]{3,0,2,1:T(8,128)(2,1)}, u32[]{:S(2)}, u32[]{:S(2)}) async-start(bf16[192,8,5,128]{3,0,2,1:T(8,128)(2,1)} %copy.51), calls=%async_computation.2 | async-start | bytes 3932160 | tf_op jit(solution)/shard_map/all_to_all | solution.py:40
  58.3 7.6 %copy-start.9 = (s32[16,2,3]{0,1,2:T(2,128)S(1)}, s32[16,2,3]{0,1,2:T(2,128)}, u32[]{:S(2)}) copy-start(s32[16,2,3]{0,1,2:T(2,128)} %param.23) | copy-start | bytes 1156
  58.3 7.9 %copy-start.8 = (s32[16,2,6]{0,1,2:T(2,128)S(1)}, s32[16,2,6]{0,1,2:T(2,128)}, u32[]{:S(2)}) copy-start(s32[16,2,6]{0,1,2:T(2,128)} %param.22) | copy-start | bytes 2308
  70.9 56.5 %all-to-all-start = ((bf16[192,8,5,128]{3,0,2,1:T(8,128)(2,1)}), bf16[192,8,5,128]{3,0,2,1:T(8,128)(2,1)}, u32[]{:S(2)}, u32[]{:S(2)}) async-start(bf16[192,8,5,128]{3,0,2,1:T(8,128)(2,1)} %copy.45), calls=%async_computation | async-start | bytes 3932160 | tf_op jit(solution)/shard_map/all_to_all | solution.py:38
  77.0 1.3 copy-start
  88.2 40.9 %collective-permute-start = (bf16[2,768,5,128]{3,1,2,0:T(8,128)(2,1)}, bf16[2,768,5,128]{3,1,2,0:T(8,128)(2,1)}, u32[]{:S(2)}, u32[]{:S(2)}) collective-permute-start(bf16[2,768,5,128]{3,1,2,0:T(8,128)(2,1)} %bitcast.21), channel_id=1, source_target_pairs={{0,8},{8,16},{16,24},{24,32},{32,40},{40,48},{48,56},{56,64},{64,7... | collective-permute-start | bytes 5898248 | tf_op jit(solution)/shard_map/ppermute | solution.py:19
  97.8 37.9 %collective-permute-start.1 = (bf16[2,768,5,128]{3,1,2,0:T(8,128)(2,1)}, bf16[2,768,5,128]{3,1,2,0:T(8,128)(2,1)}, u32[]{:S(2)}, u32[]{:S(2)}) collective-permute-start(bf16[2,768,5,128]{3,1,2,0:T(8,128)(2,1)} %bitcast.27), channel_id=1, source_target_pairs={{8,0},{16,8},{24,16},{32,24},{40,32},{48,40},{56,48},{64,56},{72,6... | collective-permute-start | bytes 5898248 | tf_op jit(solution)/shard_map/ppermute | solution.py:19
  107.9 61.6 %collective-permute-start.2 = (bf16[2,384,5,128]{3,1,2,0:T(8,128)(2,1)}, bf16[2,384,5,128]{3,1,2,0:T(8,128)(2,1)}, u32[]{:S(2)}, u32[]{:S(2)}) collective-permute-start(bf16[2,384,5,128]{3,1,2,0:T(8,128)(2,1)} %bitcast.30), channel_id=1, source_target_pairs={{0,16},{8,24},{16,32},{24,40},{32,48},{40,56},{48,64},{56,72},{64,... | collective-permute-start | bytes 2949128 | tf_op jit(solution)/shard_map/ppermute | solution.py:19
  114.7 5.5 %copy-start.1 = (bf16[192,8,5,128]{3,0,1,2:T(8,128)(2,1)S(1)}, bf16[192,8,5,128]{3,0,1,2:T(8,128)(2,1)}, u32[]{:S(2)}) copy-start(bf16[192,8,5,128]{3,0,1,2:T(8,128)(2,1)} %copy-done) | copy-start | bytes 5898244
  115.9 68.4 %collective-permute-start.3 = (bf16[2,384,5,128]{3,1,2,0:T(8,128)(2,1)}, bf16[2,384,5,128]{3,1,2,0:T(8,128)(2,1)S(1)}, u32[]{:S(2)}, u32[]{:S(2)}) collective-permute-start(bf16[2,384,5,128]{3,1,2,0:T(8,128)(2,1)} %bitcast.33), channel_id=1, source_target_pairs={{16,0},{24,8},{32,16},{40,24},{48,32},{56,40},{64,48},{72,56},{80,... | collective-permute-start | bytes 2949128 | tf_op jit(solution)/shard_map/ppermute | solution.py:19
  121.3 64.1 %collective-permute-start.4 = (bf16[2,128,5,128]{3,1,2,0:T(8,128)(2,1)}, bf16[2,128,5,128]{3,1,2,0:T(8,128)(2,1)}, u32[]{:S(2)}, u32[]{:S(2)}) collective-permute-start(bf16[2,128,5,128]{3,1,2,0:T(8,128)(2,1)} %get-tuple-element.91), channel_id=1, source_target_pairs={{0,32},{8,40},{16,48},{24,56},{32,64},{40,72},{48,80},{56,88},{64,... | collective-permute-start | bytes 983048 | tf_op jit(solution)/shard_map/ppermute | solution.py:19
  127.4 8.3 %copy-start.5 = (bf16[2,128,5,128]{3,1,2,0:T(8,128)(2,1)S(1)}, bf16[2,128,5,128]{3,1,2,0:T(8,128)(2,1)}, u32[]{:S(2)}) copy-start(bf16[2,128,5,128]{3,1,2,0:T(8,128)(2,1)} %get-tuple-element.89) | copy-start | bytes 983044
  129.2 58.1 %collective-permute-start.5 = (bf16[2,128,5,128]{3,1,2,0:T(8,128)(2,1)}, bf16[2,128,5,128]{3,1,2,0:T(8,128)(2,1)S(1)}, u32[]{:S(2)}, u32[]{:S(2)}) collective-permute-start(bf16[2,128,5,128]{3,1,2,0:T(8,128)(2,1)} %get-tuple-element.90), channel_id=1, source_target_pairs={{32,0},{40,8},{48,16},{56,24},{64,32},{72,40},{80,48},{88,56},{96,... | collective-permute-start | bytes 983048 | tf_op jit(solution)/shard_map/ppermute | solution.py:19
  135.7 52.4 %collective-permute-start.6 = (bf16[2,128,5,128]{3,1,2,0:T(8,128)(2,1)S(1)}, bf16[2,128,5,128]{3,1,2,0:T(8,128)(2,1)S(1)}, u32[]{:S(2)}, u32[]{:S(2)}) collective-permute-start(bf16[2,128,5,128]{3,1,2,0:T(8,128)(2,1)S(1)} %copy-done.5), channel_id=1, source_target_pairs={{0,64},{8,72},{16,80},{24,88},{32,96},{40,104},{48,112},{56,120},{... | collective-permute-start | bytes 983048 | tf_op jit(solution)/shard_map/ppermute | solution.py:19
  169.5 19.3 %collective-permute-start.7 = (bf16[2,128,5,128]{3,1,2,0:T(8,128)(2,1)S(1)}, bf16[2,128,5,128]{3,1,2,0:T(8,128)(2,1)S(1)}, u32[]{:S(2)}, u32[]{:S(2)}) collective-permute-start(bf16[2,128,5,128]{3,1,2,0:T(8,128)(2,1)S(1)} %get-tuple-element.88), channel_id=1, source_target_pairs={{64,0},{72,8},{80,16},{88,24},{96,32},{104,40},{112,48},{120,56},{... | collective-permute-start | bytes 983048 | tf_op jit(solution)/shard_map/ppermute | solution.py:19
  209.6 19.1 %copy-start.4 = (bf16[4352,5,128]{2,0,1:T(8,128)(2,1)S(1)}, bf16[4352,5,128]{2,0,1:T(8,128)(2,1)}, u32[]{:S(2)}) copy-start(bf16[4352,5,128]{2,0,1:T(8,128)(2,1)} %get-tuple-element.184) | copy-start | bytes 16711684 | tf_op jit(solution)/shard_map/while
  267.8 19.1 %copy-start.4 = (bf16[4352,5,128]{2,0,1:T(8,128)(2,1)S(1)}, bf16[4352,5,128]{2,0,1:T(8,128)(2,1)}, u32[]{:S(2)}) copy-start(bf16[4352,5,128]{2,0,1:T(8,128)(2,1)} %get-tuple-element.184) | copy-start | bytes 16711684 | tf_op jit(solution)/shard_map/while
  326.0 19.1 %copy-start.4 = (bf16[4352,5,128]{2,0,1:T(8,128)(2,1)S(1)}, bf16[4352,5,128]{2,0,1:T(8,128)(2,1)}, u32[]{:S(2)}) copy-start(bf16[4352,5,128]{2,0,1:T(8,128)(2,1)} %get-tuple-element.184) | copy-start | bytes 16711684 | tf_op jit(solution)/shard_map/while
where the time goes:
time: 428 us; the launch traced here: 420 us
  matrix products  117 us (27%)
  local copies, waits for them, and re-layouts  80.9 us (19%)
  other arithmetic  69.6 us (16%)
  waiting for transfers between devices  60.6 us (14%)
  starting transfers between devices  42.5 us (10%)
  blocking collectives  40.6 us (9%)
  between operations  8.06 us (2%)
    dot_general x3, matrix products, one_block(): jnp.einsum('qhd,khd->hqk', block, keys_all, preferred_element_type=jnp.fl...  60 us
    reduce_sum x3, other arithmetic, one_block(): totals = jnp.sum(expo, axis=-1, keepdims=True)  57.2 us
    dot_general x3, matrix products, one_block(): jnp.einsum('hqk,khd->qhd', weights, values_all, preferred_element_type=jn...  57.2 us
    all_to_all x1, blocking collectives, on_device(): lax.all_to_all(outputs, 'head', split_axis=0, concat_axis=1, tiled=True)  40.6 us
    ppermute x8, waiting for transfers between devices, passed_along(): lax.ppermute(value, axis, [(source, source + steps) for source in range(f...  38.6 us
    ppermute x8, starting transfers between devices, passed_along(): lax.ppermute(value, axis, [(source, source + steps) for source in range(f...  27.5 us
    unnamed x39, local copies, waits for them, and re-layouts  21.7 us
    all_to_all x1, waiting for transfers between devices, on_device(): lax.all_to_all(key_rows, 'head', split_axis=1, concat_axis=0, tiled=True)  19.4 us
  transfers between devices with their start and end apart: 11, of which 4 were waited for; matrix products, arithmetic and copies ran while one was open for 16% of the time, Pallas kernels for 0%

commit v1 on v0

v1 whole, which is shorter than its diff:
```python
import functools
import math

import jax
import jax.numpy as jnp
from jax import lax
from jax.experimental import pallas as pl
from jax.experimental.pallas import tpu as pltpu
from jax.sharding import PartitionSpec as P

MESH = pl.DeviceIdType.MESH
HEADS = 40
HD = 128
BLK = 128
EPSILON = 1e-06
NEGATIVE = -1e30
LOG2E = math.log2(math.e)

FRAMES = 16
MEMBERS = 8
PER = HEADS // MEMBERS
TOKENS = 192
S = TOKENS * MEMBERS
NB = S // BLK
WIDTH = HEADS * HD
SEGMENTS = ((1, 0, 6, 0), (1, 1, 6, 6), (2, 0, 3, 12), (2, 1, 3, 15), (4, 0, 1, 18), (4, 1, 1, 19), (8, 0, 1, 20), (8, 1, 1, 20))
KEPT = 21
KEYS = (NB + KEPT) * BLK
CHUNK = 11
TQ = 512
NORM_ROWS = 32


def nt_dot(a, b):
    return lax.dot_general(a, b, (((1,), (1,)), ((), ())), preferred_element_type=jnp.float32)


def reaches(frame, distance, direction):
    room = frame if direction == 0 else FRAMES - 1 - frame
    return jnp.minimum(room // distance, 1)


def first_block(frame, segment):
    at = NB
    for distance, direction, count, _ in SEGMENTS[:segment]:
        if distance < 8:
            at = at + count * reaches(frame, distance, direction)
    return at


def kernel(
    q_hbm, k_hbm, v_hbm, q_gain, k_gain, keep_one, keep_two, keep_four, keep_eight,
    out_hbm,
    q_in, k_in, v_in, q_norm, k_norm, queries, pairs, stage, kept, heads_out,
    load_sem, own_sem, a2a_send, a2a_recv, kept_send, kept_recv, out_send, out_recv,
):
    frame = lax.axis_index("tm")
    member = lax.axis_index("head")
    keeps = {1: keep_one, 2: keep_two, 4: keep_four, 8: keep_eight}

    def y_hi(f):
        return (f // 2) % 2

    def flip(m, bits):
        total = 0
        for b in (1, 2, 4):
            x = (m // b) % 2 + (bits // b) % 2
            total = total + b * (x % 2)
        return total

    def group_of(f, m):
        return flip(m, 4 * y_hi(f))

    mine = group_of(frame, member)
    partners = [flip(member, j) for j in range(MEMBERS)]
    their_groups = [group_of(frame, p) for p in partners]

    def rows_of(m):
        return pl.ds(pl.multiple_of(m * TOKENS, 64), TOKENS)

    loads = [
        pltpu.make_async_copy(v_hbm.at[0], v_in, load_sem.at[0]),
        pltpu.make_async_copy(k_hbm.at[0], k_in, load_sem.at[1]),
        pltpu.make_async_copy(q_hbm.at[0], q_in, load_sem.at[2]),
    ]
    for load in loads:
        load.start()

    first_idle = (NB + 11) * BLK
    for h in range(PER):
        for t in range(2):
            pairs[h, t, first_idle:, :] = jnp.zeros((KEYS - first_idle, HD), jnp.bfloat16)

    def kept_links(f):
        links = []
        for distance, direction, count, at in SEGMENTS:
            sign = 1 if direction == 0 else -1
            to = f + sign * distance
            source = f - sign * distance
            sends = jnp.logical_and(to >= 0, to < FRAMES)
            takes = jnp.logical_and(source >= 0, source < FRAMES)
            to_in = jnp.clip(to, 0, FRAMES - 1)
            links.append((sends, takes, to_in, flip(member, 4 * ((y_hi(to_in) + y_hi(f)) % 2))))
        return links

    links = kept_links(frame)

    barrier = pltpu.get_barrier_semaphore()
    for j in range(1, MEMBERS):
        pl.semaphore_signal(barrier, inc=1, device_id=(frame, partners[j]), device_id_type=MESH)
    expected = MEMBERS - 1
    for sends, takes, to, peer in links:
        @pl.when(sends)
        def _():
            pl.semaphore_signal(barrier, inc=1, device_id=(to, peer), device_id_type=MESH)

    for distance, direction, _, _ in SEGMENTS:
        expected = expected + reaches(frame, distance, 1 - direction)
    pl.semaphore_wait(barrier, expected)

    def lanes_of(head):
        return pl.ds(pl.multiple_of(head * HD, HD), HD)

    def exchange(t, h, j):
        head = their_groups[j] * PER + h
        if t == 0:
            source, target = v_in.at[:, lanes_of(head)], pairs.at[h, 1, rows_of(member)]
        elif t == 1:
            source, target = k_norm.at[head], pairs.at[h, 0, rows_of(member)]
        else:
            source, target = q_norm.at[head], queries.at[h, rows_of(member)]
        if j == 0:
            return pltpu.make_async_copy(source, target, own_sem.at[t, h])
        return pltpu.make_async_remote_copy(
            source, target, a2a_send.at[t, h, j - 1], a2a_recv.at[t, h, j - 1],
            device_id=(frame, partners[j]), device_id_type=MESH,
        )

    def arrival(t, h, j):
        rows = rows_of(partners[j])
        target = (pairs.at[h, 1, rows], pairs.at[h, 0, rows], queries.at[h, rows])[t]
        return pltpu.make_async_copy(target, target, a2a_recv.at[t, h, j - 1])

    def start_exchange(t, h):
        for j in range(1, MEMBERS):
            exchange(t, h, j).start()
        exchange(t, h, 0).start()

    def wait_exchange(t, h):
        exchange(t, h, 0).wait()
        for j in range(1, MEMBERS):
            arrival(t, h, j).wait()

    def normalise(source, gain, target):
        scale = gain[...]

        def some_rows(i, carry):
            rows = pl.ds(pl.multiple_of(i * NORM_ROWS, NORM_ROWS), NORM_ROWS)
            wide = source[rows, :].astype(jnp.float32)
            meansq = jnp.mean(wide * wide, axis=-1, keepdims=True)
            normed = (wide * lax.rsqrt(meansq + EPSILON) * scale).astype(jnp.bfloat16)
            for head in range(HEADS):
                target[head, rows, :] = normed[:, head * HD : (head + 1) * HD]
            return carry

        lax.fori_loop(0, TOKENS // NORM_ROWS, some_rows, 0)

    def kept_copy(segment, h):
        distance, direction, count, at = SEGMENTS[segment]
        _, _, to, peer = links[segment]
        start = pl.multiple_of(first_block(to, segment) * BLK, BLK)
        return pltpu.make_async_remote_copy(
            kept.at[h, :, pl.ds(at * BLK, count * BLK)], pairs.at[h, :, pl.ds(start, count * BLK)],
            kept_send.at[h, segment], kept_recv.at[h, segment],
            device_id=(to, peer), device_id_type=MESH,
        )

    def kept_arrival(segment, h):
        count = SEGMENTS[segment][2]
        start = pl.multiple_of(first_block(frame, segment) * BLK, BLK)
        target = pairs.at[h, :, pl.ds(start, count * BLK)]
        return pltpu.make_async_copy(target, target, kept_recv.at[h, segment])

    def send_kept(h):
        for t in range(2):
            stage[t] = pairs[h, t, :S, :].reshape(NB, BLK, HD)
        for segment, (distance, direction, count, at) in enumerate(SEGMENTS):
            sends, _, to, _ = links[segment]

            @pl.when(sends)
            def _():
                for i in range(count):
                    block = keeps[distance][to, direction, i]
                    for t in range(2):
                        kept[h, t, (at + i) * BLK : (at + i + 1) * BLK, :] = stage[t, block]
                kept_copy(segment, h).start()

    def wait_kept(h):
        for segment in range(len(SEGMENTS)):
            @pl.when(links[segment][1])
            def _():
                kept_arrival(segment, h).wait()

    usable_blocks = first_block(frame, len(SEGMENTS)) + 1

    def attend(h):
        scale = LOG2E / math.sqrt(HD)

        def some_queries(i, carry):
            rows = pl.ds(pl.multiple_of(i * TQ, TQ), TQ)
            q = queries[h, rows, :]
            top = jnp.full((TQ, HD), NEGATIVE, jnp.float32)
            total = jnp.zeros((TQ, HD), jnp.float32)
            summed = jnp.zeros((TQ, HD), jnp.float32)
            for chunk in range((NB + KEPT) // CHUNK):
                keys = slice(chunk * CHUNK * BLK, (chunk + 1) * CHUNK * BLK)
                scores = nt_dot(q, pairs[h, 0, keys, :])
                parts = []
                for b in range(CHUNK):
                    part = scores[:, b * BLK : (b + 1) * BLK]
                    if chunk * CHUNK + b >= NB + 11:
                        part = part + jnp.where(chunk * CHUNK + b < usable_blocks, 0.0, NEGATIVE)
                    parts.append(part)
                peak = functools.reduce(jnp.maximum, parts)
                above = jnp.maximum(top, jnp.max(peak, axis=1, keepdims=True) * scale)
                fade = jnp.exp2(top - above)
                weights = jnp.concatenate(
                    [jnp.exp2(part * scale - above).astype(jnp.bfloat16) for part in parts], axis=1
                )
                wide = jnp.concatenate(
                    [pairs[h, 1, keys, :], jnp.ones((CHUNK * BLK, HD), jnp.bfloat16)], axis=1
                )
                product = jnp.dot(weights, wide, preferred_element_type=jnp.float32)
                summed = summed * fade + product[:, :HD]
                total = total * fade + product[:, HD:]
                top = above
            heads_out[h, rows, :] = (summed / total).astype(jnp.bfloat16)
            return carry

        lax.fori_loop(0, S // TQ, some_queries, 0)

    def give_back(h, j):
        lanes = lanes_of(mine * PER + h)
        if j == 0:
            return pltpu.make_async_copy(
                heads_out.at[h, rows_of(member)], out_hbm.at[0, :, lanes], own_sem.at[3, h]
            )
        return pltpu.make_async_remote_copy(
            heads_out.at[h, rows_of(partners[j])], out_hbm.at[0, :, lanes],
            out_send.at[h, j - 1], out_recv.at[h, j - 1],
            device_id=(frame, partners[j]), device_id_type=MESH,
        )

    def returned(h, j):
        target = out_hbm.at[0, :, lanes_of(their_groups[j] * PER + h)]
        return pltpu.make_async_copy(target, target, out_recv.at[h, j - 1])

    loads[0].wait()
    start_exchange(0, 0)
    loads[1].wait()
    normalise(k_in, k_gain, k_norm)
    start_exchange(1, 0)
    loads[2].wait()
    normalise(q_in, q_gain, q_norm)
    start_exchange(2, 0)
    for t in range(3):
        start_exchange(t, 1)
    wait_exchange(0, 0)
    wait_exchange(1, 0)
    send_kept(0)

    def step(h, carry):
        @pl.when(h + 2 < PER)
        def _():
            for t in range(3):
                start_exchange(t, h + 2)

        @pl.when(h + 1 < PER)
        def _():
            wait_exchange(0, h + 1)
            wait_exchange(1, h + 1)
            send_kept(h + 1)

        wait_exchange(2, h)
        wait_kept(h)
        attend(h)
        for j in range(MEMBERS):
            give_back(h, j).start()
        return carry

    lax.fori_loop(0, PER, step, 0)

    def finish(h, carry):
        for j in range(1, MEMBERS):
            for t in range(3):
                exchange(t, h, j).wait_send()
            give_back(h, j).wait_send()
            returned(h, j).wait()
        give_back(h, 0).wait()
        for segment in range(len(SEGMENTS)):
            @pl.when(links[segment][0])
            def _():
                kept_copy(segment, h).wait_send()
        return carry

    lax.fori_loop(0, PER, finish, 0)


def on_device(q_in, k_in, v_in, q_gain, k_gain, keep_one, keep_two, keep_four, keep_eight):
    hbm = pl.BlockSpec(memory_space=pl.ANY)
    vmem = pl.BlockSpec(memory_space=pltpu.VMEM)
    smem = pl.BlockSpec(memory_space=pltpu.SMEM)
    bf16 = jnp.bfloat16
    dma = pltpu.SemaphoreType.DMA
    return pl.pallas_call(
        kernel,
        out_shape=jax.ShapeDtypeStruct((1, TOKENS, WIDTH), bf16),
        in_specs=[hbm, hbm, hbm, vmem, vmem, smem, smem, smem, smem],
        out_specs=hbm,
        scratch_shapes=[
            pltpu.VMEM((TOKENS, WIDTH), bf16),
            pltpu.VMEM((TOKENS, WIDTH), bf16),
            pltpu.VMEM((TOKENS, WIDTH), bf16),
            pltpu.VMEM((HEADS, TOKENS, HD), bf16),
            pltpu.VMEM((HEADS, TOKENS, HD), bf16),
            pltpu.VMEM((PER, S, HD), bf16),
            pltpu.VMEM((PER, 2, KEYS, HD), bf16),
            pltpu.VMEM((2, NB, BLK, HD), bf16),
            pltpu.VMEM((PER, 2, (KEPT + 1) * BLK, HD), bf16),
            pltpu.VMEM((PER, S, HD), bf16),
            dma((3,)),
            dma((4, PER)),
            dma((3, PER, MEMBERS - 1)),
            dma((3, PER, MEMBERS - 1)),
            dma((PER, len(SEGMENTS))),
            dma((PER, len(SEGMENTS))),
            dma((PER, MEMBERS - 1)),
            dma((PER, MEMBERS - 1)),
        ],
        compiler_params=pltpu.CompilerParams(
            collective_id=0, has_side_effects=True, vmem_limit_bytes=60 * 2**20
        ),
        cost_estimate=pl.CostEstimate(
            flops=4 * S * KEYS * PER * HD, bytes_accessed=8 * TOKENS * WIDTH, transcendentals=S * KEYS * PER
        ),
        name="attend",
    )(
        q_in, k_in, v_in, q_gain.reshape(1, WIDTH), k_gain.reshape(1, WIDTH),
        keep_one, keep_two, keep_four, keep_eight,
    )


def solution(mesh):
    return jax.shard_map(
        on_device,
        mesh=mesh,
        in_specs=(P("tm", "head", None),) * 3 + (P(),) * 6,
        out_specs=P("tm", "head", None),
        check_vma=False,
    )
```

time: 428 us -> 141 us (0.33); the launches traced: 420 us -> 140 us
  Pallas kernels: 0 us -> 132 us
  matrix products: 117 us -> 0 us
  local copies, waits for them, and re-layouts: 80.9 us -> 8.4 us
  other arithmetic: 69.6 us -> 0 us
  waiting for transfers between devices: 60.6 us -> 0 us
  starting transfers between devices: 42.5 us -> 0 us
  blocking collectives: 40.6 us -> 0 us
  between operations: 8.06 us -> 0.01 us
    pallas_call x0 -> x1, Pallas kernels: none -> 132 us  [on_device(): pl.pallas_call(kernel, out_shape=jax.ShapeDtypeStruct((1, TOKENS, WIDTH),...]
    dot_general x6 -> x0, matrix products: 117 us -> none  [the longest x3 60 us: one_block(): jnp.einsum('qhd,khd->hqk', block, keys_all, preferred_element_type=jnp.fl...]
    reduce_sum x5 -> x0, other arithmetic: 58.2 us -> none  [the longest x3 57.2 us: one_block(): totals = jnp.sum(expo, axis=-1, keepdims=True)]
    all_to_all x1 -> x0, blocking collectives: 40.6 us -> none  [on_device(): lax.all_to_all(outputs, 'head', split_axis=0, concat_axis=1, tiled=True)]
    ppermute x8 -> x0, waiting for transfers between devices: 38.6 us -> none  [passed_along(): lax.ppermute(value, axis, [(source, source + steps) for source in range(f...]
    ppermute x8 -> x0, starting transfers between devices: 27.5 us -> none  [passed_along(): lax.ppermute(value, axis, [(source, source + steps) for source in range(f...]
    all_to_all x3 -> x0, waiting for transfers between devices: 22.1 us -> none  [the longest x1 19.4 us: on_device(): lax.all_to_all(key_rows, 'head', split_axis=1, concat_axis=0, tiled=True)]
    all_to_all x3 -> x0, starting transfers between devices: 15 us -> none  [the longest x1 6.33 us: on_device(): lax.all_to_all(key_rows, 'head', split_axis=1, concat_axis=0, tiled=True)]
  transfers between devices with their start and end apart: 11 -> 0, of which waited for: 4 -> 0; matrix products, arithmetic and copies ran while one was open for 16% -> 0% of each run, Pallas kernels for 0% -> 0%
where the time goes in v1:
time: 141 us; the launch traced here: 140 us
  Pallas kernels  132 us (94%)
  local copies, waits for them, and re-layouts  8.4 us (6%)
    pallas_call x1, Pallas kernels, on_device(): pl.pallas_call(kernel, out_shape=jax.ShapeDtypeStruct((1, TOKENS, WIDTH),...  132 us
    unnamed x5, local copies, waits for them, and re-layouts  8.4 us

profile of v1, /device:TPU:2, one launch (start us, length us, event | category | flops | bytes accessed | tf_op | source)
XLA Modules:
  0.0 140.0 jit_solution(2077331882165113851)
XLA Ops:
  0.0 1.4 copy.10.keep_one
  1.4 1.4 copy.11.keep_two
  2.7 1.4 copy.12.keep_four
  4.1 1.4 copy.13.keep_eight
  5.5 131.6 %attend.1 = bf16[1,192,5120]{2,1,0:T(8,128)(2,1)} custom-call(bf16[1,192,5120]{2,1,0:T(8,128)(2,1)} %q_hbm.1, bf16[1,192,5120]{2,1,0:T(8,128)(2,1)} %k_hbm.1, bf16[1,192,5120]{2,1,0:T(8,128)(2,1)} %v_hbm.1, f32[1,5120]{1,0:T(1,128)} %bitcast.2, f32[1,5120]{1,0:T(1,128)} %bitcast.3, s32[16,2,6]{2,1,0:T(2,128)} %copy.10.keep_one, s32[16,2,3]{2,1,0:T(2,128)} %copy.11.keep_two, ...), custom_call_target="tpu_custom_call" | custom-call | flops 16609443840 | bytes 7864320 | tf_op jit(solution)/shard_map/attend/pallas_call | solution.py:315
  137.0 2.9 %copy.15 = bf16[1,192,5120]{2,1,0:T(8,128)(2,1)} copy(bf16[1,192,5120]{2,1,0:T(8,128)(2,1)} %attend.1) | data formatting | bytes 3932160

commit v2 on v1

v2 whole, which is shorter than its diff:
```python
import functools
import math

import jax
import jax.numpy as jnp
from jax import lax
from jax.experimental import pallas as pl
from jax.experimental.pallas import tpu as pltpu
from jax.sharding import PartitionSpec as P

MESH = pl.DeviceIdType.MESH
HEADS = 40
HD = 128
BLK = 128
EPSILON = 1e-06
NEGATIVE = -1e30
LOG2E = math.log2(math.e)

FRAMES = 16
MEMBERS = 8
PER = HEADS // MEMBERS
TOKENS = 192
S = TOKENS * MEMBERS
NB = S // BLK
WIDTH = HEADS * HD
SEGMENTS = ((1, 0, 6, 0), (1, 1, 6, 6), (2, 0, 3, 12), (2, 1, 3, 15), (4, 0, 1, 18), (4, 1, 1, 19), (8, 0, 1, 20), (8, 1, 1, 20))
KEPT = 21
UNITS = 5
ORDER = (0, 1, 2, 3, 4, 5, 6, 7)
KEYS = (NB + KEPT) * BLK
TQ = 512
TILES = S // TQ
CHUNKS = ((NB, NB + 11), (NB + 11, NB + KEPT))
SCALE = LOG2E / math.sqrt(HD)
NORM_ROWS = 32


def nt_dot(a, b):
    return lax.dot_general(a, b, (((1,), (1,)), ((), ())), preferred_element_type=jnp.float32)


def reaches(frame, distance, direction):
    room = frame if direction == 0 else FRAMES - 1 - frame
    return jnp.minimum(room // distance, 1)


def first_block(frame, segment):
    at = NB
    for distance, direction, count, _ in SEGMENTS[:segment]:
        if distance < 8:
            at = at + count * reaches(frame, distance, direction)
    return at


def kernel(
    q_hbm, k_hbm, v_hbm, q_gain, k_gain, keep_one, keep_two, keep_four, keep_eight,
    out_hbm,
    q_in, k_in, v_in, q_norm, k_norm, queries, pairs, stage, kept, heads_out, running,
    load_sem, own_sem, a2a_send, a2a_recv, kept_send, kept_recv, out_send, out_recv,
):
    frame = lax.axis_index("tm")
    member = lax.axis_index("head")
    plane, role, core = frame // 4, (frame // 2) % 2, frame % 2
    keeps = {1: keep_one, 2: keep_two, 4: keep_four, 8: keep_eight}

    def flip(m, bits):
        total = 0
        for b in (1, 2, 4):
            x = (m // b) % 2 + (bits // b) % 2
            total = total + b * (x % 2)
        return total

    roles = [(role + other) % 2 for other in range(2)]
    members = [flip(member, j) for j in range(MEMBERS)]

    def place(i):
        return 4 * plane + 2 * roles[i // MEMBERS] + core, members[i % MEMBERS]

    def head_at(s, i):
        its_role = roles[i // MEMBERS]
        group = flip(members[i % MEMBERS], 4 * its_role)
        return group * PER + (2 * its_role + s if s < 2 else 4)

    def unit_of(s, i):
        return 2 * s + i // MEMBERS if s < 2 else 4

    def partners_of(unit):
        first = MEMBERS * (unit % 2)
        return range(first, first + MEMBERS)

    def frame_of(unit):
        return 4 * plane + 2 * ((role + unit % 2) % 2) + core

    def rows_of(m):
        return pl.ds(pl.multiple_of(m * TOKENS, 64), TOKENS)

    def lanes_of(head):
        return pl.ds(pl.multiple_of(head * HD, HD), HD)

    loads = [
        pltpu.make_async_copy(v_hbm.at[0], v_in, load_sem.at[0]),
        pltpu.make_async_copy(k_hbm.at[0], k_in, load_sem.at[1]),
        pltpu.make_async_copy(q_hbm.at[0], q_in, load_sem.at[2]),
    ]
    for load in loads:
        load.start()

    barrier = pltpu.get_barrier_semaphore()

    def greet(device):
        pl.semaphore_signal(barrier, inc=1, device_id=device, device_id_type=MESH)

    first_idle = (NB + 11) * BLK
    for u in range(UNITS):
        for t in range(2):
            pairs[u, t, first_idle:, :] = jnp.zeros((KEYS - first_idle, HD), jnp.bfloat16)

    for i in range(1, 2 * MEMBERS):
        greet(place(i))
    greet((frame + 1 - 2 * core, member))
    expected = 2 * MEMBERS
    near = jnp.minimum(3 - plane, 1), jnp.minimum(plane, 1)
    far = (3 - plane) // 2, plane // 2
    far = jnp.minimum(far[0], 1), jnp.minimum(far[1], 1)
    across = core * near[0] + (1 - core) * near[1]
    side = 2 * core - 1
    meets = [
        (near[0], frame + 4), (near[1], frame - 4), (far[0], frame + 8), (far[1], frame - 8),
        (across, frame + 4 * side - side),
    ]
    for there, to in meets:
        expected = expected + there

        @pl.when(there > 0)
        def _():
            greet((to, member))

    def target_frame(f, segment):
        distance, direction, _, _ = SEGMENTS[segment]
        return f + distance if direction == 0 else f - distance

    def clipped(f):
        return jnp.clip(f, 0, FRAMES - 1)

    def role_of(f):
        return (f // 2) % 2

    def single_place(to):
        return to, flip(member, 4 * ((role_of(to) + role) % 2))

    for segment, (distance, direction, _, _) in enumerate(SEGMENTS):
        to = target_frame(frame, segment)
        there = reaches(frame, distance, 1 - direction)
        expected = expected + there

        @pl.when(there > 0)
        def _():
            greet(single_place(clipped(to)))

    pl.semaphore_wait(barrier, expected)

    def exchange(t, s, i):
        head, unit = head_at(s, i), unit_of(s, i)
        if t == 0:
            source, target = v_in.at[:, lanes_of(head)], pairs.at[unit, 1, rows_of(member)]
        elif t == 1:
            source, target = k_norm.at[head], pairs.at[unit, 0, rows_of(member)]
        else:
            source, target = q_norm.at[head], queries.at[unit, rows_of(member)]
        if i == 0:
            return pltpu.make_async_copy(source, target, own_sem.at[t, s])
        return pltpu.make_async_remote_copy(
            source, target, a2a_send.at[t, s, i], a2a_recv.at[t, s, i],
            device_id=place(i), device_id_type=MESH,
        )

    def start_exchange(t, unit):
        for i in partners_of(unit):
            exchange(t, unit // 2, i).start()

    def wait_exchange(t, unit):
        s = unit // 2
        for i in partners_of(unit):
            if i == 0:
                exchange(t, s, 0).wait()
                continue
            rows = rows_of(members[i % MEMBERS])
            target = (pairs.at[unit, 1, rows], pairs.at[unit, 0, rows], queries.at[unit, rows])[t]
            pltpu.make_async_copy(target, target, a2a_recv.at[t, s, i]).wait()

    def normalise(source, gain, target):
        scale = gain[...]

        def some_rows(i, carry):
            rows = pl.ds(pl.multiple_of(i * NORM_ROWS, NORM_ROWS), NORM_ROWS)
            wide = source[rows, :].astype(jnp.float32)
            meansq = jnp.mean(wide * wide, axis=-1, keepdims=True)
            normed = (wide * lax.rsqrt(meansq + EPSILON) * scale).astype(jnp.bfloat16)
            for head in range(HEADS):
                target[head, rows, :] = normed[:, head * HD : (head + 1) * HD]
            return carry

        lax.fori_loop(0, TOKENS // NORM_ROWS, some_rows, 0)

    def inside(f, segment, unit):
        distance, direction, _, _ = SEGMENTS[segment]
        there = reaches(f, distance, 1 - direction)
        if distance != 2 or unit == 4:
            return there, None
        here = 1 - role_of(f) if direction == 0 else role_of(f)
        return there * (1 - here), here

    def kept_copy(segment, unit, piece=None):
        _, _, count, at = SEGMENTS[segment]
        to = clipped(target_frame(frame_of(unit), segment))
        start = pl.multiple_of(first_block(to, segment) * BLK, BLK)
        if unit == 4:
            device, its_unit = single_place(to), 4
        else:
            device = (4 * (to // 4) + 2 * role + to % 2, member)
            its_unit = 2 * (unit // 2) + (role_of(to) + role) % 2
        source, target = kept.at[unit, :, pl.ds(at * BLK, count * BLK)], pairs.at[its_unit, :, pl.ds(start, count * BLK)]
        if piece is not None:
            i, t = piece
            source = kept.at[unit, t, pl.ds((at + i) * BLK, BLK)]
            target = pairs.at[its_unit, t, pl.ds(pl.multiple_of(start + i * BLK, BLK), BLK)]
        return pltpu.make_async_remote_copy(
            source, target,
            kept_send.at[unit, segment], kept_recv.at[its_unit, segment],
            device_id=device, device_id_type=MESH,
        )

    def send_kept(unit):
        f = frame_of(unit)
        for t in range(2):
            stage[t] = pairs[unit, t, :S, :].reshape(NB, BLK, HD)
        for segment in ORDER:
            distance, direction, count, at = SEGMENTS[segment]
            there, here = inside(f, segment, unit)
            to = clipped(target_frame(f, segment))

            def chosen(i):
                keep = keeps[distance]
                return keep[i, direction, to] if count > 1 else keep[direction, i, to]

            @pl.when(there > 0)
            def _():
                for i in range(count):
                    block = chosen(i)
                    for t in range(2):
                        kept[unit, t, (at + i) * BLK : (at + i + 1) * BLK, :] = stage[t, block]
                for i in range(count):
                    for t in range(2):
                        kept_copy(segment, unit, (i, t)).start()

            if here is not None:
                start = first_block(to, segment)

                @pl.when(here > 0)
                def _():
                    for i in range(count):
                        block = chosen(i)
                        rows = pl.ds(pl.multiple_of((start + i) * BLK, BLK), BLK)
                        for t in range(2):
                            pairs[unit ^ 1, t, rows, :] = stage[t, block]

    def wait_kept(unit):
        f = frame_of(unit)
        for segment, (distance, direction, count, _) in enumerate(SEGMENTS):
            there = reaches(f, distance, direction)
            if distance == 2 and unit != 4:
                there = there * (1 - role_of(f) if direction == 0 else role_of(f))

            @pl.when(there > 0)
            def _():
                start = pl.multiple_of(first_block(f, segment) * BLK, BLK)
                target = pairs.at[unit, :, pl.ds(start, count * BLK)]
                pltpu.make_async_copy(target, target, kept_recv.at[unit, segment]).wait()

    def weigh(q, u, first, last, usable):
        scores = nt_dot(q, pairs[u, 0, first * BLK : last * BLK, :])
        parts = []
        for b in range(first, last):
            part = scores[:, (b - first) * BLK : (b - first + 1) * BLK]
            if b >= NB + 11:
                part = part + jnp.where(b < usable, 0.0, NEGATIVE)
            parts.append(part)
        peak = functools.reduce(jnp.maximum, parts)
        return parts, jnp.max(peak, axis=1, keepdims=True) * SCALE

    def gather(parts, above, u, first, last):
        weights = jnp.concatenate(
            [jnp.exp2(part * SCALE - above).astype(jnp.bfloat16) for part in parts], axis=1
        )
        wide = jnp.concatenate(
            [pairs[u, 1, first * BLK : last * BLK, :], jnp.ones(((last - first) * BLK, HD), jnp.bfloat16)], axis=1
        )
        product = jnp.dot(weights, wide, preferred_element_type=jnp.float32)
        return product[:, :HD], product[:, HD:]

    def tile_rows(i):
        return pl.ds(pl.multiple_of(i * TQ, TQ), TQ)

    def attend_own(u, n, i):
        rows = tile_rows(i)
        parts, peak = weigh(queries[u, rows, :], u, 0, NB, NB)
        above = jnp.broadcast_to(peak, (TQ, HD))
        running[n, 0, rows, :] = above
        running[n, 1, rows, :], running[n, 2, rows, :] = gather(parts, above, u, 0, NB)

    def attend_kept(u, n, i):
        rows = tile_rows(i)
        usable = first_block(frame_of(u), len(SEGMENTS)) + 1
        q = queries[u, rows, :]
        top, summed, total = running[n, 0, rows, :], running[n, 1, rows, :], running[n, 2, rows, :]
        for first, last in CHUNKS:
            parts, peak = weigh(q, u, first, last, usable)
            above = jnp.maximum(top, peak)
            fade = jnp.exp2(top - above)
            product, sums = gather(parts, above, u, first, last)
            summed = summed * fade + product
            total = total * fade + sums
            top = above
        heads_out[u, rows, :] = (summed / total).astype(jnp.bfloat16)

    def give_back(s, i):
        unit, lanes = unit_of(s, i), lanes_of(head_at(s, 0))
        source, target = heads_out.at[unit, rows_of(members[i % MEMBERS])], out_hbm.at[0, :, lanes]
        if i == 0:
            return pltpu.make_async_copy(source, target, own_sem.at[3, s])
        return pltpu.make_async_remote_copy(
            source, target, out_send.at[s, i], out_recv.at[s, i], device_id=place(i), device_id_type=MESH
        )

    def give(unit):
        for i in partners_of(unit):
            give_back(unit // 2, i).start()

    def take(*tensors):
        for t, unit in tensors:
            wait_exchange(t, unit)

    loads[0].wait()
    start_exchange(0, 0)
    loads[1].wait()
    normalise(k_in, k_gain, k_norm)
    start_exchange(1, 0)
    loads[2].wait()
    normalise(q_in, q_gain, q_norm)
    start_exchange(2, 0)
    for unit in range(1, UNITS):
        for t in range(3):
            start_exchange(t, unit)

    own, others = 0, 1
    values_keys = lambda unit: take((0, unit), (1, unit))

    def before_own_1():
        values_keys(1)
        send_kept(1)
        take((2, 1))

    def before_others_1():
        give(0)
        wait_kept(1)
        values_keys(2)
        send_kept(2)

    def late_others_1():
        values_keys(3)
        send_kept(3)

    def before_own_2():
        give(1)
        take((2, 2))

    def late_others_2():
        values_keys(4)
        send_kept(4)

    def before_others_3():
        give(2)
        wait_kept(3)

    def before_own_4():
        give(3)
        take((2, 4))

    values_keys(0)
    send_kept(0)
    phases = [
        (own, 0, 0, TILES, lambda: take((2, 0))),
        (own, 1, 0, TILES, before_own_1),
        (others, 0, 0, TILES, lambda: wait_kept(0)),
        (others, 1, 0, TILES - 1, before_others_1),
        (others, 1, TILES - 1, TILES, late_others_1),
        (own, 2, 0, TILES, before_own_2),
        (own, 3, 0, TILES, lambda: take((2, 3))),
        (others, 2, 0, 1, lambda: wait_kept(2)),
        (others, 2, 1, TILES, late_others_2),
        (others, 3, 0, TILES, before_others_3),
        (own, 4, 0, TILES, before_own_4),
        (others, 4, 0, TILES, lambda: wait_kept(4)),
    ]

    def pick(n, column):
        return functools.reduce(lambda v, k: jnp.where(n == k, phases[k][column], v), range(len(phases)), 0)

    def phase(n, carry):
        kind, unit, first, last = (pick(n, column) for column in range(4))
        for k, (_, _, _, _, todo) in enumerate(phases):
            if todo is not None:
                pl.when(n == k)(todo)

        def own_tile(i, c):
            attend_own(unit, unit, i)
            return c

        def kept_tile(i, c):
            attend_kept(unit, unit, i)
            return c

        lax.fori_loop(first, jnp.where(kind == own, last, first), own_tile, 0)
        lax.fori_loop(first, jnp.where(kind == own, first, last), kept_tile, 0)
        return carry

    lax.fori_loop(0, len(phases), phase, 0)
    give(4)

    for unit in range(UNITS):
        s = unit // 2
        for i in partners_of(unit):
            if i == 0:
                give_back(s, 0).wait()
                continue
            for t in range(3):
                exchange(t, s, i).wait_send()
            give_back(s, i).wait_send()
            target = out_hbm.at[0, :, lanes_of(head_at(s, i))]
            pltpu.make_async_copy(target, target, out_recv.at[s, i]).wait()
    for unit in range(UNITS):
        for segment in range(len(SEGMENTS)):
            @pl.when(inside(frame_of(unit), segment, unit)[0] > 0)
            def _():
                kept_copy(segment, unit).wait_send()


def on_device(q_in, k_in, v_in, q_gain, k_gain, keep_one, keep_two, keep_four, keep_eight):
    hbm = pl.BlockSpec(memory_space=pl.ANY)
    vmem = pl.BlockSpec(memory_space=pltpu.VMEM)
    smem = pl.BlockSpec(memory_space=pltpu.SMEM)
    bf16 = jnp.bfloat16
    dma = pltpu.SemaphoreType.DMA
    return pl.pallas_call(
        kernel,
        out_shape=jax.ShapeDtypeStruct((1, TOKENS, WIDTH), bf16),
        in_specs=[hbm, hbm, hbm, vmem, vmem, smem, smem, smem, smem],
        out_specs=hbm,
        scratch_shapes=[
            pltpu.VMEM((TOKENS, WIDTH), bf16),
            pltpu.VMEM((TOKENS, WIDTH), bf16),
            pltpu.VMEM((TOKENS, WIDTH), bf16),
            pltpu.VMEM((HEADS, TOKENS, HD), bf16),
            pltpu.VMEM((HEADS, TOKENS, HD), bf16),
            pltpu.VMEM((UNITS, S, HD), bf16),
            pltpu.VMEM((UNITS, 2, KEYS, HD), bf16),
            pltpu.VMEM((2, NB, BLK, HD), bf16),
            pltpu.VMEM((UNITS, 2, KEPT * BLK, HD), bf16),
            pltpu.VMEM((UNITS, S, HD), bf16),
            pltpu.VMEM((UNITS, 3, S, HD), jnp.float32),
            dma((3,)),
            dma((4, 3)),
            dma((3, 3, 2 * MEMBERS)),
            dma((3, 3, 2 * MEMBERS)),
            dma((UNITS, len(SEGMENTS))),
            dma((UNITS, len(SEGMENTS))),
            dma((3, 2 * MEMBERS)),
            dma((3, 2 * MEMBERS)),
        ],
        compiler_params=pltpu.CompilerParams(
            collective_id=0, has_side_effects=True, vmem_limit_bytes=60 * 2**20
        ),
        cost_estimate=pl.CostEstimate(
            flops=4 * S * KEYS * PER * HD, bytes_accessed=8 * TOKENS * WIDTH, transcendentals=S * KEYS * PER
        ),
        name="attend",
    )(
        q_in, k_in, v_in, q_gain.reshape(1, WIDTH), k_gain.reshape(1, WIDTH),
        keep_one.transpose(2, 1, 0), keep_two.transpose(2, 1, 0),
        keep_four.transpose(1, 2, 0), keep_eight.transpose(1, 2, 0),
    )


def solution(mesh):
    return jax.shard_map(
        on_device,
        mesh=mesh,
        in_specs=(P("tm", "head", None),) * 3 + (P(),) * 6,
        out_specs=P("tm", "head", None),
        check_vma=False,
    )
```

time: 141 us -> 122 us (0.87)
  Pallas kernels: 132 us -> 119 us
  local copies, waits for them, and re-layouts: 8.4 us -> 2.94 us
    pallas_call x1, Pallas kernels: 132 us -> 119 us  [on_device(): pl.pallas_call(kernel, out_shape=jax.ShapeDtypeStruct((1, TOKENS, WIDTH),...]
    unnamed x5 -> x1, local copies, waits for them, and re-layouts: 8.4 us -> 2.94 us
where the time goes in v2:
time: 122 us
  Pallas kernels  119 us (98%)
  local copies, waits for them, and re-layouts  2.94 us (2%)
    pallas_call x1, Pallas kernels, on_device(): pl.pallas_call(kernel, out_shape=jax.ShapeDtypeStruct((1, TOKENS, WIDTH),...  119 us
    unnamed x1, local copies, waits for them, and re-layouts  2.94 us

profile of v2, /device:TPU:2, one launch (start us, length us, event | category | flops | bytes accessed | tf_op | source)
XLA Modules:
  0.0 121.6 jit_solution(11721862067242951934)
XLA Ops:
  0.0 118.6 %attend.1 = bf16[1,192,5120]{2,1,0:T(8,128)(2,1)} custom-call(bf16[1,192,5120]{2,1,0:T(8,128)(2,1)} %q_hbm.1, bf16[1,192,5120]{2,1,0:T(8,128)(2,1)} %k_hbm.1, bf16[1,192,5120]{2,1,0:T(8,128)(2,1)} %v_hbm.1, f32[1,5120]{1,0:T(1,128)} %bitcast.6, f32[1,5120]{1,0:T(1,128)} %bitcast.7, s32[6,2,16]{2,1,0:T(2,128)} %bitcast.8, s32[3,2,16]{2,1,0:T(2,128)} %bitcast.9, ...), custom_call_target="tpu_custom_call" | custom-call | flops 16609443840 | bytes 7864320 | tf_op jit(solution)/shard_map/attend/pallas_call | solution.py:454
  118.6 2.9 %copy.11 = bf16[1,192,5120]{2,1,0:T(8,128)(2,1)} copy(bf16[1,192,5120]{2,1,0:T(8,128)(2,1)} %attend.1) | data formatting | bytes 3932160

commit v3 on v2

--- a/solution.py
+++ b/solution.py
@@ -41,7 +41,7 @@
 
 def reaches(frame, distance, direction):
     room = frame if direction == 0 else FRAMES - 1 - frame
-    return jnp.minimum(room // distance, 1)
+    return jnp.minimum(lax.div(room, distance), 1)
 
 
 def first_block(frame, segment):
@@ -60,17 +60,20 @@
 ):
     frame = lax.axis_index("tm")
     member = lax.axis_index("head")
-    plane, role, core = frame // 4, (frame // 2) % 2, frame % 2
+    plane, role, core = lax.div(frame, 4), lax.rem(lax.div(frame, 2), 2), lax.rem(frame, 2)
     keeps = {1: keep_one, 2: keep_two, 4: keep_four, 8: keep_eight}
+
+    def bit(m, b):
+        return (m // b) % 2 if isinstance(m, int) else lax.rem(lax.div(m, b), 2)
 
     def flip(m, bits):
         total = 0
         for b in (1, 2, 4):
-            x = (m // b) % 2 + (bits // b) % 2
-            total = total + b * (x % 2)
+            x = bit(m, b) + bit(bits, b)
+            total = total + b * lax.rem(x, 2)
         return total
 
-    roles = [(role + other) % 2 for other in range(2)]
+    roles = [lax.rem(role + other, 2) for other in range(2)]
     members = [flip(member, j) for j in range(MEMBERS)]
 
     def place(i):
@@ -143,7 +146,7 @@
         return jnp.clip(f, 0, FRAMES - 1)
 
     def role_of(f):
-        return (f // 2) % 2
+        return lax.rem(lax.div(f, 2), 2)
 
     def single_place(to):
         return to, flip(member, 4 * ((role_of(to) + role) % 2))
@@ -170,7 +173,7 @@
         if i == 0:
             return pltpu.make_async_copy(source, target, own_sem.at[t, s])
         return pltpu.make_async_remote_copy(
-            source, target, a2a_send.at[t, s, i], a2a_recv.at[t, s, i],
+            source, target, a2a_send.at[t], a2a_recv.at[t, unit],
             device_id=place(i), device_id_type=MESH,
         )
 
@@ -179,14 +182,12 @@
             exchange(t, unit // 2, i).start()
 
     def wait_exchange(t, unit):
-        s = unit // 2
-        for i in partners_of(unit):
-            if i == 0:
-                exchange(t, s, 0).wait()
-                continue
-            rows = rows_of(members[i % MEMBERS])
-            target = (pairs.at[unit, 1, rows], pairs.at[unit, 0, rows], queries.at[unit, rows])[t]
-            pltpu.make_async_copy(target, target, a2a_recv.at[t, s, i]).wait()
+        rows = S
+        if unit % 2 == 0:
+            exchange(t, unit // 2, 0).wait()
+            rows = S - TOKENS
+        some = heads_out.at[0, pl.ds(0, rows)]
+        pltpu.make_async_copy(some, some, a2a_recv.at[t, unit]).wait()
 
     def normalise(source, gain, target):
         scale = gain[...]
@@ -210,7 +211,7 @@
         here = 1 - role_of(f) if direction == 0 else role_of(f)
         return there * (1 - here), here
 
-    def kept_copy(segment, unit, piece=None):
+    def kept_copy(segment, unit):
         _, _, count, at = SEGMENTS[segment]
         to = clipped(target_frame(frame_of(unit), segment))
         start = pl.multiple_of(first_block(to, segment) * BLK, BLK)
@@ -220,10 +221,6 @@
             device = (4 * (to // 4) + 2 * role + to % 2, member)
             its_unit = 2 * (unit // 2) + (role_of(to) + role) % 2
         source, target = kept.at[unit, :, pl.ds(at * BLK, count * BLK)], pairs.at[its_unit, :, pl.ds(start, count * BLK)]
-        if piece is not None:
-            i, t = piece
-            source = kept.at[unit, t, pl.ds((at + i) * BLK, BLK)]
-            target = pairs.at[its_unit, t, pl.ds(pl.multiple_of(start + i * BLK, BLK), BLK)]
         return pltpu.make_async_remote_copy(
             source, target,
             kept_send.at[unit, segment], kept_recv.at[its_unit, segment],
@@ -249,9 +246,7 @@
                     block = chosen(i)
                     for t in range(2):
                         kept[unit, t, (at + i) * BLK : (at + i + 1) * BLK, :] = stage[t, block]
-                for i in range(count):
-                    for t in range(2):
-                        kept_copy(segment, unit, (i, t)).start()
+                kept_copy(segment, unit).start()
 
             if here is not None:
                 start = first_block(to, segment)
@@ -329,7 +324,7 @@
         if i == 0:
             return pltpu.make_async_copy(source, target, own_sem.at[3, s])
         return pltpu.make_async_remote_copy(
-            source, target, out_send.at[s, i], out_recv.at[s, i], device_id=place(i), device_id_type=MESH
+            source, target, out_send.at[0], out_recv.at[0], device_id=place(i), device_id_type=MESH
         )
 
     def give(unit):
@@ -340,67 +335,82 @@
         for t, unit in tensors:
             wait_exchange(t, unit)
 
+    def give_rows(unit, first, last):
+        s, other = unit // 2, unit % 2
+        for m in range(first, last):
+            j = flip(member, m)
+            source = heads_out.at[unit, m * TOKENS : (m + 1) * TOKENS]
+            target = out_hbm.at[0, :, lanes_of(head_at(s, 0))]
+
+            def send():
+                pltpu.make_async_remote_copy(
+                    source, target, out_send.at[0], out_recv.at[0],
+                    device_id=(4 * plane + 2 * roles[other] + core, m), device_id_type=MESH,
+                ).start()
+
+            if other:
+                send()
+                continue
+            pl.when(j > 0)(send)
+
+            @pl.when(j == 0)
+            def _():
+                pltpu.make_async_copy(source, target, own_sem.at[3, s]).start()
+
     loads[0].wait()
-    start_exchange(0, 0)
+    start_exchange(0, 4)
+    start_exchange(0, 1)
     loads[1].wait()
     normalise(k_in, k_gain, k_norm)
-    start_exchange(1, 0)
+    start_exchange(1, 4)
+    start_exchange(1, 1)
     loads[2].wait()
     normalise(q_in, q_gain, q_norm)
-    start_exchange(2, 0)
-    for unit in range(1, UNITS):
+    start_exchange(2, 4)
+    start_exchange(2, 1)
+    for t in range(3):
+        start_exchange(t, 0)
+    take((0, 4), (1, 4))
+    send_kept(4)
+    for unit in (3, 2):
         for t in range(3):
             start_exchange(t, unit)
 
     own, others = 0, 1
     values_keys = lambda unit: take((0, unit), (1, unit))
 
-    def before_own_1():
-        values_keys(1)
-        send_kept(1)
-        take((2, 1))
-
-    def before_others_1():
+    def before_own(unit):
+        values_keys(unit)
+        send_kept(unit)
+        take((2, unit))
+
+    def before_others(unit, done):
+        give(done)
+        wait_kept(unit)
+
+    def meanwhile(unit):
+        values_keys(unit)
+        send_kept(unit)
+
+    def before_own_3():
         give(0)
-        wait_kept(1)
-        values_keys(2)
-        send_kept(2)
-
-    def late_others_1():
-        values_keys(3)
-        send_kept(3)
-
-    def before_own_2():
-        give(1)
-        take((2, 2))
-
-    def late_others_2():
-        values_keys(4)
-        send_kept(4)
-
-    def before_others_3():
-        give(2)
-        wait_kept(3)
-
-    def before_own_4():
-        give(3)
-        take((2, 4))
-
-    values_keys(0)
-    send_kept(0)
+        take((2, 3))
+
     phases = [
-        (own, 0, 0, TILES, lambda: take((2, 0))),
-        (own, 1, 0, TILES, before_own_1),
-        (others, 0, 0, TILES, lambda: wait_kept(0)),
-        (others, 1, 0, TILES - 1, before_others_1),
-        (others, 1, TILES - 1, TILES, late_others_1),
-        (own, 2, 0, TILES, before_own_2),
-        (own, 3, 0, TILES, lambda: take((2, 3))),
-        (others, 2, 0, 1, lambda: wait_kept(2)),
-        (others, 2, 1, TILES, late_others_2),
-        (others, 3, 0, TILES, before_others_3),
-        (own, 4, 0, TILES, before_own_4),
+        (own, 4, 0, TILES, lambda: take((2, 4))),
+        (own, 1, 0, TILES, lambda: before_own(1)),
+        (own, 0, 0, TILES, lambda: before_own(0)),
         (others, 4, 0, TILES, lambda: wait_kept(4)),
+        (others, 1, 0, 1, lambda: before_others(1, 4)),
+        (others, 1, 1, TILES, lambda: meanwhile(3)),
+        (others, 0, 0, 1, lambda: before_others(0, 1)),
+        (others, 0, 1, TILES, lambda: meanwhile(2)),
+        (own, 3, 0, TILES, before_own_3),
+        (own, 2, 0, TILES, lambda: take((2, 2))),
+        (others, 3, 0, TILES, lambda: wait_kept(3)),
+        (others, 2, 0, 1, lambda: before_others(2, 3)),
+        (others, 2, 1, 2, lambda: give_rows(2, 0, 2)),
+        (others, 2, 2, TILES, lambda: give_rows(2, 2, 5)),
     ]
 
     def pick(n, column):
@@ -425,19 +435,13 @@
         return carry
 
     lax.fori_loop(0, len(phases), phase, 0)
-    give(4)
-
-    for unit in range(UNITS):
-        s = unit // 2
-        for i in partners_of(unit):
-            if i == 0:
-                give_back(s, 0).wait()
-                continue
-            for t in range(3):
-                exchange(t, s, i).wait_send()
-            give_back(s, i).wait_send()
-            target = out_hbm.at[0, :, lanes_of(head_at(s, i))]
-            pltpu.make_async_copy(target, target, out_recv.at[s, i]).wait()
+    give_rows(2, 5, 8)
+
+    for s in range(3):
+        give_back(s, 0).wait()
+    copies = k_norm.at[pl.ds(0, MEMBERS * UNITS - 3)]
+    for semaphore in (a2a_send.at[0], a2a_send.at[1], a2a_send.at[2], out_send.at[0], out_recv.at[0]):
+        pltpu.make_async_copy(copies, copies, semaphore).wait()
     for unit in range(UNITS):
         for segment in range(len(SEGMENTS)):
             @pl.when(inside(frame_of(unit), segment, unit)[0] > 0)
@@ -470,12 +474,12 @@
             pltpu.VMEM((UNITS, 3, S, HD), jnp.float32),
             dma((3,)),
             dma((4, 3)),
-            dma((3, 3, 2 * MEMBERS)),
-            dma((3, 3, 2 * MEMBERS)),
+            dma((3,)),
+            dma((3, UNITS)),
             dma((UNITS, len(SEGMENTS))),
             dma((UNITS, len(SEGMENTS))),
-            dma((3, 2 * MEMBERS)),
-            dma((3, 2 * MEMBERS)),
+            dma((1,)),
+            dma((1,)),
         ],
         compiler_params=pltpu.CompilerParams(
             collective_id=0, has_side_effects=True, vmem_limit_bytes=60 * 2**20

time: 122 us -> 119 us (0.975)
  Pallas kernels: 119 us -> 116 us
    pallas_call x1, Pallas kernels: 119 us -> 116 us  [on_device(): pl.pallas_call(kernel, out_shape=jax.ShapeDtypeStruct((1, TOKENS, WIDTH),...]
where the time goes in v3:
time: 119 us
  Pallas kernels  116 us (97%)
  local copies, waits for them, and re-layouts  2.94 us (2%)
    pallas_call x1, Pallas kernels, on_device(): pl.pallas_call(kernel, out_shape=jax.ShapeDtypeStruct((1, TOKENS, WIDTH),...  116 us
    unnamed x1, local copies, waits for them, and re-layouts  2.94 us

profile of v3, /device:TPU:2, one launch (start us, length us, event | category | flops | bytes accessed | tf_op | source)
XLA Modules:
  0.0 118.9 jit_solution(12725109666977582327)
XLA Ops:
  0.0 115.9 %attend.1 = bf16[1,192,5120]{2,1,0:T(8,128)(2,1)} custom-call(bf16[1,192,5120]{2,1,0:T(8,128)(2,1)} %q_hbm.1, bf16[1,192,5120]{2,1,0:T(8,128)(2,1)} %k_hbm.1, bf16[1,192,5120]{2,1,0:T(8,128)(2,1)} %v_hbm.1, f32[1,5120]{1,0:T(1,128)} %bitcast.6, f32[1,5120]{1,0:T(1,128)} %bitcast.7, s32[6,2,16]{2,1,0:T(2,128)} %bitcast.8, s32[3,2,16]{2,1,0:T(2,128)} %bitcast.9, ...), custom_call_target="tpu_custom_call" | custom-call | flops 16609443840 | bytes 7864320 | tf_op jit(solution)/shard_map/attend/pallas_call | solution.py:458
  115.9 2.9 %copy.11 = bf16[1,192,5120]{2,1,0:T(8,128)(2,1)} copy(bf16[1,192,5120]{2,1,0:T(8,128)(2,1)} %attend.1) | data formatting | bytes 3932160

commit v4 on v3

--- a/solution.py
+++ b/solution.py
@@ -28,7 +28,7 @@
 UNITS = 5
 ORDER = (0, 1, 2, 3, 4, 5, 6, 7)
 KEYS = (NB + KEPT) * BLK
-TQ = 512
+TQ = 768
 TILES = S // TQ
 CHUNKS = ((NB, NB + 11), (NB + 11, NB + KEPT))
 SCALE = LOG2E / math.sqrt(HD)
@@ -55,7 +55,7 @@
 def kernel(
     q_hbm, k_hbm, v_hbm, q_gain, k_gain, keep_one, keep_two, keep_four, keep_eight,
     out_hbm,
-    q_in, k_in, v_in, q_norm, k_norm, queries, pairs, stage, kept, heads_out, running,
+    q_in, k_in, q_norm, k_norm, queries, pairs, stage, kept, heads_out, running,
     load_sem, own_sem, a2a_send, a2a_recv, kept_send, kept_recv, out_send, out_recv,
 ):
     frame = lax.axis_index("tm")
@@ -101,9 +101,8 @@
         return pl.ds(pl.multiple_of(head * HD, HD), HD)
 
     loads = [
-        pltpu.make_async_copy(v_hbm.at[0], v_in, load_sem.at[0]),
-        pltpu.make_async_copy(k_hbm.at[0], k_in, load_sem.at[1]),
-        pltpu.make_async_copy(q_hbm.at[0], q_in, load_sem.at[2]),
+        pltpu.make_async_copy(k_hbm.at[0], k_in, load_sem.at[0]),
+        pltpu.make_async_copy(q_hbm.at[0], q_in, load_sem.at[1]),
     ]
     for load in loads:
         load.start()
@@ -165,7 +164,7 @@
     def exchange(t, s, i):
         head, unit = head_at(s, i), unit_of(s, i)
         if t == 0:
-            source, target = v_in.at[:, lanes_of(head)], pairs.at[unit, 1, rows_of(member)]
+            source, target = v_hbm.at[0, :, lanes_of(head)], pairs.at[unit, 1, rows_of(member)]
         elif t == 1:
             source, target = k_norm.at[head], pairs.at[unit, 0, rows_of(member)]
         else:
@@ -357,14 +356,13 @@
             def _():
                 pltpu.make_async_copy(source, target, own_sem.at[3, s]).start()
 
-    loads[0].wait()
     start_exchange(0, 4)
     start_exchange(0, 1)
-    loads[1].wait()
+    loads[0].wait()
     normalise(k_in, k_gain, k_norm)
     start_exchange(1, 4)
     start_exchange(1, 1)
-    loads[2].wait()
+    loads[1].wait()
     normalise(q_in, q_gain, q_norm)
     start_exchange(2, 4)
     start_exchange(2, 1)
@@ -409,8 +407,7 @@
         (own, 2, 0, TILES, lambda: take((2, 2))),
         (others, 3, 0, TILES, lambda: wait_kept(3)),
         (others, 2, 0, 1, lambda: before_others(2, 3)),
-        (others, 2, 1, 2, lambda: give_rows(2, 0, 2)),
-        (others, 2, 2, TILES, lambda: give_rows(2, 2, 5)),
+        (others, 2, 1, TILES, lambda: give_rows(2, 0, 4)),
     ]
 
     def pick(n, column):
@@ -435,7 +432,7 @@
         return carry
 
     lax.fori_loop(0, len(phases), phase, 0)
-    give_rows(2, 5, 8)
+    give_rows(2, 4, 8)
 
     for s in range(3):
         give_back(s, 0).wait()
@@ -457,11 +454,10 @@
     dma = pltpu.SemaphoreType.DMA
     return pl.pallas_call(
         kernel,
-        out_shape=jax.ShapeDtypeStruct((1, TOKENS, WIDTH), bf16),
+        out_shape=pltpu.VMEM((1, TOKENS, WIDTH), bf16),
         in_specs=[hbm, hbm, hbm, vmem, vmem, smem, smem, smem, smem],
-        out_specs=hbm,
+        out_specs=vmem,
         scratch_shapes=[
-            pltpu.VMEM((TOKENS, WIDTH), bf16),
             pltpu.VMEM((TOKENS, WIDTH), bf16),
             pltpu.VMEM((TOKENS, WIDTH), bf16),
             pltpu.VMEM((HEADS, TOKENS, HD), bf16),
@@ -472,7 +468,7 @@
             pltpu.VMEM((UNITS, 2, KEPT * BLK, HD), bf16),
             pltpu.VMEM((UNITS, S, HD), bf16),
             pltpu.VMEM((UNITS, 3, S, HD), jnp.float32),
-            dma((3,)),
+            dma((2,)),
             dma((4, 3)),
             dma((3,)),
             dma((3, UNITS)),
@@ -482,7 +478,7 @@
             dma((1,)),
         ],
         compiler_params=pltpu.CompilerParams(
-            collective_id=0, has_side_effects=True, vmem_limit_bytes=60 * 2**20
+            collective_id=0, has_side_effects=True, vmem_limit_bytes=56 * 2**20
         ),
         cost_estimate=pl.CostEstimate(
             flops=4 * S * KEYS * PER * HD, bytes_accessed=8 * TOKENS * WIDTH, transcendentals=S * KEYS * PER

time: 119 us -> 116 us (0.975)
  Pallas kernels: 116 us -> 114 us
  local copies, waits for them, and re-layouts: 2.94 us -> 1.27 us
    pallas_call x1, Pallas kernels: 116 us -> 114 us  [on_device(): pl.pallas_call(kernel, out_shape=pltpu.VMEM((1, TOKENS, WIDTH), bf16), in...]
    unnamed x1, local copies, waits for them, and re-layouts: 2.94 us -> 1.27 us
where the time goes in v4:
time: 116 us; the launch traced here: 115 us
  Pallas kernels  114 us (98%)
  local copies, waits for them, and re-layouts  1.27 us (1%)
    pallas_call x1, Pallas kernels, on_device(): pl.pallas_call(kernel, out_shape=pltpu.VMEM((1, TOKENS, WIDTH), bf16), in...  114 us

profile of v4, /device:TPU:2, one launch (start us, length us, event | category | flops | bytes accessed | tf_op | source)
XLA Modules:
  0.0 114.8 jit_solution(10758719592109471026)
XLA Ops:
  0.0 113.6 %attend.1 = bf16[1,192,5120]{2,1,0:T(8,128)(2,1)S(1)} custom-call(bf16[1,192,5120]{2,1,0:T(8,128)(2,1)} %q_hbm.1, bf16[1,192,5120]{2,1,0:T(8,128)(2,1)} %k_hbm.1, bf16[1,192,5120]{2,1,0:T(8,128)(2,1)} %v_hbm.1, f32[1,5120]{1,0:T(1,128)} %bitcast.6, f32[1,5120]{1,0:T(1,128)} %bitcast.7, s32[6,2,16]{2,1,0:T(2,128)} %bitcast.8, s32[3,2,16]{2,1,0:T(2,128)} %bitcast.9, ...), custom_call_target="tpu_custom_call" | custom-call | flops 16609443840 | bytes 7864320 | tf_op jit(solution)/shard_map/attend/pallas_call | solution.py:455
  113.6 1.3 %copy.11 = bf16[1,192,5120]{2,1,0:T(8,128)(2,1)} copy(bf16[1,192,5120]{2,1,0:T(8,128)(2,1)S(1)} %attend.1) | data formatting | bytes 3932160

commit v5 on v4

--- a/solution.py
+++ b/solution.py
@@ -368,11 +368,11 @@
     start_exchange(2, 1)
     for t in range(3):
         start_exchange(t, 0)
-    take((0, 4), (1, 4))
-    send_kept(4)
     for unit in (3, 2):
         for t in range(3):
             start_exchange(t, unit)
+    take((0, 4), (1, 4))
+    send_kept(4)
 
     own, others = 0, 1
     values_keys = lambda unit: take((0, unit), (1, unit))
@@ -386,26 +386,33 @@
         give(done)
         wait_kept(unit)
 
-    def meanwhile(unit):
+    def serve(unit):
         values_keys(unit)
         send_kept(unit)
 
+    def before_others_1():
+        serve(3)
+        wait_kept(1)
+
     def before_own_3():
+        give(1)
+        take((2, 3))
+
+    def before_own_2():
         give(0)
-        take((2, 3))
+        take((2, 2))
 
     phases = [
         (own, 4, 0, TILES, lambda: take((2, 4))),
         (own, 1, 0, TILES, lambda: before_own(1)),
         (own, 0, 0, TILES, lambda: before_own(0)),
+        (others, 1, 0, TILES, before_others_1),
+        (own, 3, 0, TILES, before_own_3),
+        (others, 0, 0, 1, lambda: wait_kept(0)),
+        (others, 0, 1, TILES, lambda: serve(2)),
+        (own, 2, 0, TILES, before_own_2),
         (others, 4, 0, TILES, lambda: wait_kept(4)),
-        (others, 1, 0, 1, lambda: before_others(1, 4)),
-        (others, 1, 1, TILES, lambda: meanwhile(3)),
-        (others, 0, 0, 1, lambda: before_others(0, 1)),
-        (others, 0, 1, TILES, lambda: meanwhile(2)),
-        (own, 3, 0, TILES, before_own_3),
-        (own, 2, 0, TILES, lambda: take((2, 2))),
-        (others, 3, 0, TILES, lambda: wait_kept(3)),
+        (others, 3, 0, TILES, lambda: before_others(3, 4)),
         (others, 2, 0, 1, lambda: before_others(2, 3)),
         (others, 2, 1, TILES, lambda: give_rows(2, 0, 4)),
     ]

time: 116 us -> 114 us (0.983)
  Pallas kernels: 114 us -> 112 us
    pallas_call x1, Pallas kernels: 114 us -> 112 us  [on_device(): pl.pallas_call(kernel, out_shape=pltpu.VMEM((1, TOKENS, WIDTH), bf16), in...]
where the time goes in v5:
time: 114 us; the launch traced here: 113 us
  Pallas kernels  112 us (98%)
  local copies, waits for them, and re-layouts  1.27 us (1%)
    pallas_call x1, Pallas kernels, on_device(): pl.pallas_call(kernel, out_shape=pltpu.VMEM((1, TOKENS, WIDTH), bf16), in...  112 us

profile of v5, /device:TPU:2, one launch (start us, length us, event | category | flops | bytes accessed | tf_op | source)
XLA Modules:
  0.0 113.2 jit_solution(6378142636964640347)
XLA Ops:
  0.0 111.9 %attend.1 = bf16[1,192,5120]{2,1,0:T(8,128)(2,1)S(1)} custom-call(bf16[1,192,5120]{2,1,0:T(8,128)(2,1)} %q_hbm.1, bf16[1,192,5120]{2,1,0:T(8,128)(2,1)} %k_hbm.1, bf16[1,192,5120]{2,1,0:T(8,128)(2,1)} %v_hbm.1, f32[1,5120]{1,0:T(1,128)} %bitcast.6, f32[1,5120]{1,0:T(1,128)} %bitcast.7, s32[6,2,16]{2,1,0:T(2,128)} %bitcast.8, s32[3,2,16]{2,1,0:T(2,128)} %bitcast.9, ...), custom_call_target="tpu_custom_call" | custom-call | flops 16609443840 | bytes 7864320 | tf_op jit(solution)/shard_map/attend/pallas_call | solution.py:462
  111.9 1.3 %copy.11 = bf16[1,192,5120]{2,1,0:T(8,128)(2,1)} copy(bf16[1,192,5120]{2,1,0:T(8,128)(2,1)S(1)} %attend.1) | data formatting | bytes 3932160

commit v6 on v5

--- a/solution.py
+++ b/solution.py
@@ -386,17 +386,10 @@
         give(done)
         wait_kept(unit)
 
-    def serve(unit):
-        values_keys(unit)
-        send_kept(unit)
-
-    def before_others_1():
-        serve(3)
-        wait_kept(1)
-
-    def before_own_3():
-        give(1)
-        take((2, 3))
+    def midway():
+        for unit in (2, 3):
+            values_keys(unit)
+            send_kept(unit)
 
     def before_own_2():
         give(0)
@@ -406,11 +399,11 @@
         (own, 4, 0, TILES, lambda: take((2, 4))),
         (own, 1, 0, TILES, lambda: before_own(1)),
         (own, 0, 0, TILES, lambda: before_own(0)),
-        (others, 1, 0, TILES, before_others_1),
-        (own, 3, 0, TILES, before_own_3),
-        (others, 0, 0, 1, lambda: wait_kept(0)),
-        (others, 0, 1, TILES, lambda: serve(2)),
+        (others, 1, 0, TILES, lambda: wait_kept(1)),
+        (others, 0, 0, 1, lambda: before_others(0, 1)),
+        (others, 0, 1, TILES, midway),
         (own, 2, 0, TILES, before_own_2),
+        (own, 3, 0, TILES, lambda: take((2, 3))),
         (others, 4, 0, TILES, lambda: wait_kept(4)),
         (others, 3, 0, TILES, lambda: before_others(3, 4)),
         (others, 2, 0, 1, lambda: before_others(2, 3)),

time: 114 us -> 113 us (level); the launches traced: 113 us -> 111 us
  Pallas kernels: 112 us -> 110 us
    pallas_call x1, Pallas kernels: 112 us -> 110 us  [on_device(): pl.pallas_call(kernel, out_shape=pltpu.VMEM((1, TOKENS, WIDTH), bf16), in...]
where the time goes in v6:
time: 113 us; the launch traced here: 111 us
  Pallas kernels  110 us (97%)
  local copies, waits for them, and re-layouts  1.27 us (1%)
    pallas_call x1, Pallas kernels, on_device(): pl.pallas_call(kernel, out_shape=pltpu.VMEM((1, TOKENS, WIDTH), bf16), in...  110 us

profile of v6, /device:TPU:2, one launch (start us, length us, event | category | flops | bytes accessed | tf_op | source)
XLA Modules:
  0.0 110.8 jit_solution(3624239652398137947)
XLA Ops:
  0.0 109.5 %attend.1 = bf16[1,192,5120]{2,1,0:T(8,128)(2,1)S(1)} custom-call(bf16[1,192,5120]{2,1,0:T(8,128)(2,1)} %q_hbm.1, bf16[1,192,5120]{2,1,0:T(8,128)(2,1)} %k_hbm.1, bf16[1,192,5120]{2,1,0:T(8,128)(2,1)} %v_hbm.1, f32[1,5120]{1,0:T(1,128)} %bitcast.6, f32[1,5120]{1,0:T(1,128)} %bitcast.7, s32[6,2,16]{2,1,0:T(2,128)} %bitcast.8, s32[3,2,16]{2,1,0:T(2,128)} %bitcast.9, ...), custom_call_target="tpu_custom_call" | custom-call | flops 16609443840 | bytes 7864320 | tf_op jit(solution)/shard_map/attend/pallas_call | solution.py:455
  109.6 1.3 %copy.11 = bf16[1,192,5120]{2,1,0:T(8,128)(2,1)} copy(bf16[1,192,5120]{2,1,0:T(8,128)(2,1)S(1)} %attend.1) | data formatting | bytes 3932160
